TPU v7x, 32 devices: a whole 2x2x4 slice. The times are simulated.
32 devices in a mesh: tm: 4 (over y, core), space: 8 (over z, x).
Axes of the slice: x: 2, y: 2, z: 4, core: 2. Of those that a mesh axis runs over, the one named last changes fastest.
Arguments:
- features: bfloat16 [8, 64, 128, 256], P('tm', 'space'), may hold values from -6 to 6
- clip_frames: int32 [2], replicated, may hold values from 1 to 4, as said below
- band_maps: int32 [3, 8], replicated, may hold values from 0 to 7, each once within a row
- gain_one: float32 [256], replicated, may hold values from 0.1 to 1.9
- conv_one: bfloat16 [3, 3, 3, 256, 256], replicated, may hold values from -0.078125 to 0.078125
- gain_two: float32 [256], replicated, may hold values from 0.1 to 1.9
- conv_two: bfloat16 [3, 3, 3, 256, 256], replicated, may hold values from -0.078125 to 0.078125
- gain_out: float32 [256], replicated, may hold values from 0.1 to 1.9
- latent_weight: bfloat16 [256, 16], replicated, may hold values from -0.375 to 0.375
- embed_weight: bfloat16 [64, 3072], replicated, may hold values from -0.75 to 0.75
Outputs:
- tokens_fine: bfloat16 [8, 8, 32, 8, 3072], P('tm', 'space')
- tokens_mid: bfloat16 [8, 8, 16, 4, 3072], P('tm', 'space')
- tokens_coarse: bfloat16 [8, 8, 8, 2, 3072], P('tm', 'space')
Inputs may be any that keep to these rules, and one draw needn't show every extreme that they name: `clip_frames`: one clip has exactly 4 real frames and the other fewer. `band_maps`: each row is a permutation of the 8 bands.
All inputs are finite; a program needn't handle non-finite values.
Results may differ from a plain program's by a relative error of at most 0.011.
Values may be sent and summed in bfloat16 or wider, within the bound.
A program may use at most 128 MiB of HBM per device.

v0:
```python
import jax
import jax.numpy as jnp
from jax import lax
from jax.sharding import PartitionSpec as P


def from_behind(array, axis, by):
    peers = lax.axis_size(axis)
    pairs = [(i, i + by) for i in range(peers) if 0 <= i + by < peers]
    return lax.ppermute(array, axis, pairs)


def with_halo(cells, sides, width):
    for axis, dim in sides:
        count = lax.axis_size(axis)
        ends = count - 1
        head = lax.slice_in_dim(cells, 0, width, axis=dim)
        tail = lax.slice_in_dim(cells, cells.shape[dim] - width, cells.shape[dim], axis=dim)
        cells = jnp.concatenate(
            [
                lax.ppermute(tail, axis, [(i, (i + 1) % count) for i in range(ends)]),
                cells,
                lax.ppermute(head, axis, [((i + 1) % count, i) for i in range(ends)]),
            ],
            axis=dim,
        )
    return cells


def activate(stream, gain_vec):
    values = stream.astype(jnp.float32)
    meansq = jnp.mean(values * values, axis=-1, keepdims=True)
    return jax.nn.silu(values * lax.rsqrt(meansq + 1e-06) * gain_vec)


def causal_conv(bordered, weight, frame_ids, clip_len):
    out_frames = bordered.shape[0] - 2
    out_rows = bordered.shape[1] - 2
    col_count = bordered.shape[2]
    channels = bordered.shape[3]
    widened = jnp.pad(bordered, ((0, 0), (0, 0), (1, 1), (0, 0)))
    position = jnp.mod(frame_ids, clip_len)
    running = jnp.zeros((out_frames, out_rows, col_count, weight.shape[-1]), jnp.float32)
    for tap_time in range(3):
        keep_mask = (position >= 2 - tap_time)[:, None, None, None]
        for tap_row in range(3):
            window_rows = widened[tap_time : tap_time + out_frames, tap_row : tap_row + out_rows]
            stacked = jnp.concatenate(
                [
                    window_rows[:, :, 0:col_count],
                    window_rows[:, :, 1 : col_count + 1],
                    window_rows[:, :, 2 : col_count + 2],
                ],
                axis=-1,
            )
            stacked = jnp.where(keep_mask, stacked, jnp.zeros_like(stacked))
            kernel = weight[tap_time, tap_row].reshape(3 * channels, -1)
            running = running + jnp.einsum(
                "frwk,ko->frwo", stacked, kernel, preferred_element_type=jnp.float32
            )
    return running


def section_each(stream, gain_vec, weight, frame_ids, clip_len):
    activated = activate(stream, gain_vec).astype(jnp.bfloat16)
    earlier = from_behind(activated, "tm", 1)
    extended = jnp.concatenate([earlier, activated], axis=0)
    bordered = with_halo(extended, (("space", 1),), 1)
    update = causal_conv(bordered, weight, frame_ids, clip_len)
    return (stream.astype(jnp.float32) + update).astype(jnp.bfloat16)


def level_patches(latent, factor, band_order, valid, bands):
    frames, rows, cols, lat = latent.shape
    pooled = latent.reshape(frames, rows // factor, factor, cols // factor, factor, lat).mean(
        axis=(2, 4)
    )
    patch_rows = rows // factor // 2
    patch_cols = cols // factor // 2
    patches = pooled.reshape(frames, patch_rows, 2, patch_cols, 2, lat).transpose(0, 1, 3, 2, 4, 5)
    patches = patches.reshape(frames, patch_rows, patch_cols, 4 * lat).astype(jnp.bfloat16)
    patches = jnp.where(valid[:, None, None, None], patches, jnp.zeros_like(patches))
    grouped = patches.reshape(frames, patch_rows, bands, patch_cols // bands, 4 * lat)
    return jnp.take(grouped, band_order, axis=2).transpose(0, 2, 1, 3, 4)


def embed_tokens(grouped, embed_weight):
    embedded = jnp.einsum(
        "fbrcp,ph->fbrch", grouped, embed_weight, preferred_element_type=jnp.float32
    )
    return embedded.astype(jnp.bfloat16)


def settle(moved):
    frames, bands, rows, cols, hidden = moved.shape
    return moved.reshape(frames, 1, bands * rows, cols, hidden)


def body(
    features,
    clip_frames,
    band_maps,
    gain_one,
    conv_one,
    gain_two,
    conv_two,
    gain_out,
    latent_weight,
    embed_weight,
):
    frames_here = features.shape[0]
    clip_len = frames_here * lax.axis_size("tm") // 2
    bands = lax.axis_size("space")
    first_slot = lax.axis_index("tm") * frames_here
    frame_ids = first_slot + jnp.arange(frames_here, dtype=jnp.int32)
    stream = section_each(features, gain_one, conv_one, frame_ids, clip_len)
    stream = section_each(stream, gain_two, conv_two, frame_ids, clip_len)
    final_act = activate(stream, gain_out).astype(jnp.bfloat16)
    latent = jnp.einsum(
        "frwc,cl->frwl", final_act, latent_weight, preferred_element_type=jnp.float32
    )
    clip_ids = frame_ids // clip_len
    limits = jnp.where(clip_ids == 0, clip_frames[0], clip_frames[1])
    valid = frame_ids - clip_ids * clip_len < limits
    patch_zero = level_patches(latent, 1, band_maps[0], valid, bands)
    patch_one = level_patches(latent, 2, band_maps[1], valid, bands)
    patch_two = level_patches(latent, 4, band_maps[2], valid, bands)
    results = [
        lax.all_to_all(
            embed_tokens(patch_zero, embed_weight), "space", split_axis=1, concat_axis=1, tiled=True
        ),
        lax.all_to_all(
            embed_tokens(patch_one, embed_weight), "space", split_axis=1, concat_axis=1, tiled=True
        ),
        lax.all_to_all(
            embed_tokens(patch_two, embed_weight), "space", split_axis=1, concat_axis=1, tiled=True
        ),
    ]
    return (settle(results[0]), settle(results[1]), settle(results[2]))


def solution(mesh):
    return jax.shard_map(
        body,
        mesh=mesh,
        in_specs=(P("tm", "space", None, None), P(), P(), P(), P(), P(), P(), P(), P(), P()),
        out_specs=(
            P("tm", "space", None, None, None),
            P("tm", "space", None, None, None),
            P("tm", "space", None, None, None),
        ),
        check_vma=False,
    )
```

profile of v0, /device:TPU:1, one launch (start us, length us, event | category | flops | bytes accessed | tf_op | source)
XLA Modules:
  0.0 225.9 jit_solution(17290478257097394166)
XLA Ops:
  0.6 1.6 fusion.121
  2.3 1.9 fusion.128
  4.2 4.5 %collective-permute-start = (bf16[2,8,128,256]{3,2,1,0:T(8,128)(2,1)S(1)}, bf16[2,8,128,256]{3,2,1,0:T(8,128)(2,1)S(1)}, u32[]{:S(2)}, u32[]{:S(2)}) collective-permute-start(bf16[2,8,128,256]{3,2,1,0:T(8,128)(2,1)S(1)} %fusion.128), channel_id=1, source_target_pairs={{0,8},{8,16},{16,24},{1,9},{9,17},{17,25},{2,10},{10,18},{18,26},{... | collective-permute-start | bytes 3145736 | tf_op jit(solution)/shard_map/ppermute | solution.py:10
  8.8 11.7 %collective-permute-done = bf16[2,8,128,256]{3,2,1,0:T(8,128)(2,1)S(1)} collective-permute-done((bf16[2,8,128,256]{3,2,1,0:T(8,128)(2,1)S(1)}, bf16[2,8,128,256]{3,2,1,0:T(8,128)(2,1)S(1)}, u32[]{:S(2)}, u32[]{:S(2)}) %collective-permute-start) | collective-permute-done | bytes 1048608 | tf_op jit(solution)/shard_map/ppermute | solution.py:10
  20.5 3.1 %collective-permute-start.1 = (bf16[4,1,128,256]{3,2,1,0:T(8,128)(2,1)S(1)}, bf16[4,1,128,256]{3,2,1,0:T(8,128)(2,1)S(1)}, u32[]{:S(2)}, u32[]{:S(2)}) collective-permute-start(bf16[4,1,128,256]{3,2,1,0:T(8,128)(2,1)S(1)} %get-tuple-element.87), channel_id=1, source_target_pairs={{0,1},{1,2},{2,3},{3,4},{4,5},{5,6},{6,7},{8,9},{9,10},{10,11},{11... | collective-permute-start | bytes 786440 | tf_op jit(solution)/shard_map/ppermute | solution.py:21
  23.6 1.3 collective-permute-start.2
  24.9 3.4 %fusion.210 = (bf16[1,1,3,256,256]{4,3,2,1,0:T(8,128)(2,1)S(1)}, bf16[1,1,3,256,256]{4,3,2,1,0:T(8,128)(2,1)}, bf16[1,1,3,256,256]{4,3,2,1,0:T(8,128)(2,1)}, bf1...) fusion(bf16[3,3,3,256,256]{4,3,2,1,0:T(8,128)(2,1)} %param.14), kind=kLoop, calls=%fused_computation.288 | loop fusion | bytes 7077888 | tf_op jit(solution)/shard_map/slice | solution.py:57
  28.3 2.4 %collective-permute-done.2 = bf16[4,1,128,256]{3,2,1,0:T(8,128)(2,1)S(1)} collective-permute-done((bf16[4,1,128,256]{3,2,1,0:T(8,128)(2,1)S(1)}, bf16[4,1,128,256]{3,2,1,0:T(8,128)(2,1)S(1)}, u32[]{:S(2)}, u32[]{:S(2)}) %collective-permute-start.2) | collective-permute-done | bytes 262176 | tf_op jit(solution)/shard_map/ppermute | solution.py:23
  30.8 1.2 select_maximum_fusion.3
  32.0 7.6 %fusion.212 = (bf16[2,8,128,256]{3,2,1,0:T(8,128)(2,1)S(1)}, bf16[2,8,128,256]{3,2,1,0:T(8,128)(2,1)}, bf16[2,8,128,256]{3,2,1,0:T(8,128)(2,1)}, bf16[2,8,128,25...) fusion(bf16[4,10,130,256]{3,2,1,0:T(8,128)(2,1)S(1)} %select_ma, ...), kind=kLoop, calls=%fused_computation.290 | loop fusion | bytes 37748736 | tf_op jit(solution)/shard_map/slice | solution.py:50
  40.3 2.2 fusion.215
  43.4 1.3 fusion.8
  45.3 1.3 fusion.18
  47.0 1.3 fusion.23
  48.3 1.3 fusion.28
  49.9 1.3 fusion.38
  51.5 2.4 %fusion.33 = f32[2,8,128,256]{3,2,1,0:T(8,128)} fusion(bf16[768,256,1,1]{1,0,3,2:T(8,128)(2,1)S(1)} %bitcast.194, bf16[2,8,128,256]{3,2,1,0:T(8,128)(2,1)S(1)} %get-tuple-element.54, bf16[2,8,128,256]{3,2,1,0:T(8,128)(2,1)S(1)} %copy-done.21, bf16[2,8,128,256]{3,2,1,0:T(8,128)(2,1)S(1)} %copy-done.8, pred[2]{0:T(512)(128)(4,1)S(1)} %get-tuple-element.107), kind=kOutput, calls=%fused_computation.49 | convolution fusion | flops 816316416 | bytes 5636098 | tf_op jit(solution)/shard_map/frwk,ko->frwo/dot_general | solution.py:58
  53.9 2.2 fusion.88
  56.2 2.4 %fusion.13 = f32[2,8,128,256]{3,2,1,0:T(8,128)} fusion(bf16[768,256,1,1]{1,0,3,2:T(8,128)(2,1)S(1)} %bitcast.190, bf16[2,8,128,256]{3,2,1,0:T(8,128)(2,1)S(1)} %get-tuple-element.64, bf16[2,8,128,256]{3,2,1,0:T(8,128)(2,1)S(1)} %collective-permute-done, bf16[2,8,128,256]{3,2,1,0:T(8,128)(2,1)S(1)} %get-tuple-element.65, pred[2]{0:T(512)(128)(4,1)S(1)} %get-tuple-element.106), kind=kOutput, calls=%fused_computation.25 | convolution fusion | flops 816316416 | bytes 5636098 | tf_op jit(solution)/shard_map/frwk,ko->frwo/dot_general | solution.py:58
  58.6 4.1 %fusion.130 = (f32[2,8,128]{2,1,0:T(8,128)S(1)}, bf16[2,8,128,256]{3,2,1,0:T(8,128)(2,1)S(1)}) fusion(bf16[768,256,1,1]{1,0,3,2:T(8,128)(2,1)S(1)} %bitcast.180, bf16[2,8,128,256]{3,2,1,0:T(8,128)(2,1)S(1)} %get-tuple-element.68, bf16[2,8,128,256]{3,2,1,0:T(8,128)(2,1)S(1)} %get-tuple-element.75, bf16[2,8,128,256]{3,2,1,0:T(8,128)(2,1)S(1)} %get-tuple-element.51, ...), kind=kOutput, calls=%fused_computation.171 | convolution fusion | flops 823654400 | bytes 22421506 | tf_op jit(solution)/shard_map/frwk,ko->frwo/dot_general | solution.py:58
  63.4 5.8 %collective-permute-start.3 = (bf16[2,8,128,256]{3,2,1,0:T(8,128)(2,1)S(1)}, bf16[2,8,128,256]{3,2,1,0:T(8,128)(2,1)S(1)}, u32[]{:S(2)}, u32[]{:S(2)}) collective-permute-start(bf16[2,8,128,256]{3,2,1,0:T(8,128)(2,1)S(1)} %fusion.137), channel_id=1, source_target_pairs={{0,8},{8,16},{16,24},{1,9},{9,17},{17,25},{2,10},{10,18},{18,26},{... | collective-permute-start | bytes 3145736 | tf_op jit(solution)/shard_map/ppermute | solution.py:10
  71.1 1.7 fusion.209
  72.7 8.2 %collective-permute-done.3 = bf16[2,8,128,256]{3,2,1,0:T(8,128)(2,1)S(1)} collective-permute-done((bf16[2,8,128,256]{3,2,1,0:T(8,128)(2,1)S(1)}, bf16[2,8,128,256]{3,2,1,0:T(8,128)(2,1)S(1)}, u32[]{:S(2)}, u32[]{:S(2)}) %collective-permute-start.3) | collective-permute-done | bytes 1048608 | tf_op jit(solution)/shard_map/ppermute | solution.py:10
  81.0 4.1 %collective-permute-start.4 = (bf16[4,1,128,256]{3,2,1,0:T(8,128)(2,1)S(1)}, bf16[4,1,128,256]{3,2,1,0:T(8,128)(2,1)S(1)}, u32[]{:S(2)}, u32[]{:S(2)}) collective-permute-start(bf16[4,1,128,256]{3,2,1,0:T(8,128)(2,1)S(1)} %get-tuple-element.83), channel_id=1, source_target_pairs={{0,1},{1,2},{2,3},{3,4},{4,5},{5,6},{6,7},{8,9},{9,10},{10,11},{11... | collective-permute-start | bytes 786440 | tf_op jit(solution)/shard_map/ppermute | solution.py:21
  85.1 1.5 collective-permute-start.5
  86.6 1.3 fusion.168
  88.5 3.7 %collective-permute-done.5 = bf16[4,1,128,256]{3,2,1,0:T(8,128)(2,1)S(1)} collective-permute-done((bf16[4,1,128,256]{3,2,1,0:T(8,128)(2,1)S(1)}, bf16[4,1,128,256]{3,2,1,0:T(8,128)(2,1)S(1)}, u32[]{:S(2)}, u32[]{:S(2)}) %collective-permute-start.5) | collective-permute-done | bytes 262176 | tf_op jit(solution)/shard_map/ppermute | solution.py:23
  93.5 7.8 %fusion.211 = (bf16[2,8,128,256]{3,2,1,0:T(8,128)(2,1)S(1)}, bf16[2,8,128,256]{3,2,1,0:T(8,128)(2,1)}, bf16[2,8,128,256]{3,2,1,0:T(8,128)(2,1)}, bf16[2,8,128,25...) fusion(bf16[4,10,130,256]{3,2,1,0:T(8,128)(2,1)S(1)} %select_ma, ...), kind=kLoop, calls=%fused_computation.289 | loop fusion | bytes 37748736 | tf_op jit(solution)/shard_map/slice | solution.py:50
  104.0 1.3 fusion.78
  105.7 1.3 fusion.48
  107.0 1.3 fusion.58
  108.3 1.3 fusion.63
  109.7 1.3 fusion.68
  111.0 1.3 fusion.73
  112.6 1.3 fusion.53
  113.9 2.2 fusion.90
  116.2 3.8 %fusion.113 = (f32[2,8,128]{2,1,0:T(8,128)S(1)}, bf16[2,8,128,256]{3,2,1,0:T(8,128)(2,1)S(1)}) fusion(bf16[768,256,1,1]{1,0,3,2:T(8,128)(2,1)S(1)} %bitcast.179, bf16[2,8,128,256]{3,2,1,0:T(8,128)(2,1)S(1)} %get-tuple-element.50, bf16[2,8,128,256]{3,2,1,0:T(8,128)(2,1)S(1)} %get-tuple-element.69, bf16[2,8,128,256]{3,2,1,0:T(8,128)(2,1)S(1)} %get-tuple-element.33, ...), kind=kOutput, calls=%fused_computation.154 | convolution fusion | flops 823654400 | bytes 22421506 | tf_op jit(solution)/shard_map/frwk,ko->frwo/dot_general | solution.py:58
  124.8 4.8 %all-to-all-start.2 = ((bf16[2,8,1,2,3072]{4,3,0,2,1:T(2,128)(2,1)}), bf16[2,8,1,2,3072]{4,3,0,2,1:T(2,128)(2,1)S(1)}, u32[]{:S(2)}, u32[]{:S(2)}) async-start(bf16[2,8,1,2,3072]{4,3,0,2,1:T(2,128)(2,1)} %copy.53), calls=%async_computation.2 | async-start | bytes 393216 | tf_op jit(solution)/shard_map/all_to_all | solution.py:135
  130.6 1.5 copy.48
  132.1 4.2 %all-to-all-done.2 = bf16[2,8,1,2,3072]{4,3,0,2,1:T(2,128)(2,1)S(1)} async-done(((bf16[2,8,1,2,3072]{4,3,0,2,1:T(2,128)(2,1)}), bf16[2,8,1,2,3072]{4,3,0,2,1:T(2,128)(2,1)S(1)}, u32[]{:S(2)}, u32[]{:S(2)}) %all-to-all-start.2) | async-done | bytes 196640 | tf_op jit(solution)/shard_map/all_to_all | solution.py:135
  137.0 3.5 %all-to-all-start.1 = ((bf16[2,8,2,4,3072]{4,3,2,0,1:T(4,128)(2,1)}), bf16[2,8,2,4,3072]{4,3,2,0,1:T(4,128)(2,1)S(1)}, u32[]{:S(2)}, u32[]{:S(2)}) async-start(bf16[2,8,2,4,3072]{4,3,2,0,1:T(4,128)(2,1)} %copy.48), calls=%async_computation.1 | async-start | bytes 1572864 | tf_op jit(solution)/shard_map/all_to_all | solution.py:132
  143.0 1.9 copy.44
  144.9 7.9 %all-to-all-done.1 = bf16[2,8,2,4,3072]{4,3,2,0,1:T(4,128)(2,1)S(1)} async-done(((bf16[2,8,2,4,3072]{4,3,2,0,1:T(4,128)(2,1)}), bf16[2,8,2,4,3072]{4,3,2,0,1:T(4,128)(2,1)S(1)}, u32[]{:S(2)}, u32[]{:S(2)}) %all-to-all-start.1) | async-done | bytes 786464 | tf_op jit(solution)/shard_map/all_to_all | solution.py:132
  153.8 3.7 %all-to-all-start = ((bf16[2,8,4,8,3072]{4,3,2,0,1:T(8,128)(2,1)}), bf16[2,8,4,8,3072]{4,3,2,0,1:T(8,128)(2,1)S(1)}, u32[]{:S(2)}, u32[]{:S(2)}) async-start(bf16[2,8,4,8,3072]{4,3,2,0,1:T(8,128)(2,1)} %copy.44), calls=%async_computation | async-start | bytes 6291456 | tf_op jit(solution)/shard_map/all_to_all | solution.py:129
  157.4 1.7 copy.56
  159.2 2.3 %copy.49 = bf16[2,8,2,4,3072]{4,3,2,1,0:T(4,128)(2,1)} copy(bf16[2,8,2,4,3072]{4,3,2,0,1:T(4,128)(2,1)} %copy-done.3) | data formatting | bytes 1572864 | tf_op jit(solution)/shard_map/all_to_all | solution.py:132
  161.5 62.5 %all-to-all-done = bf16[2,8,4,8,3072]{4,3,2,0,1:T(8,128)(2,1)S(1)} async-done(((bf16[2,8,4,8,3072]{4,3,2,0,1:T(8,128)(2,1)}), bf16[2,8,4,8,3072]{4,3,2,0,1:T(8,128)(2,1)S(1)}, u32[]{:S(2)}, u32[]{:S(2)}) %all-to-all-start) | async-done | bytes 3145760 | tf_op jit(solution)/shard_map/all_to_all | solution.py:129
  224.0 2.0 copy.45
  (149 shorter events, 20.5 us)
Async XLA Ops:
  0.6 123.1 %copy-start = (bf16[64,3072]{1,0:T(8,128)(2,1)S(1)}, bf16[64,3072]{1,0:T(8,128)(2,1)}, u32[]{:S(2)}) copy-start(bf16[64,3072]{1,0:T(8,128)(2,1)} %param.19) | copy-start | bytes 1179652
  4.2 16.3 %collective-permute-start = (bf16[2,8,128,256]{3,2,1,0:T(8,128)(2,1)S(1)}, bf16[2,8,128,256]{3,2,1,0:T(8,128)(2,1)S(1)}, u32[]{:S(2)}, u32[]{:S(2)}) collective-permute-start(bf16[2,8,128,256]{3,2,1,0:T(8,128)(2,1)S(1)} %fusion.128), channel_id=1, source_target_pairs={{0,8},{8,16},{16,24},{1,9},{9,17},{17,25},{2,10},{10,18},{18,26},{... | collective-permute-start | bytes 3145736 | tf_op jit(solution)/shard_map/ppermute | solution.py:10
  8.8 45.1 %copy-start.51 = (pred[2]{0:T(512)(128)(4,1)}, pred[2]{0:T(512)(128)(4,1)S(1)}, u32[]{:S(2)}) copy-start(pred[2]{0:T(512)(128)(4,1)S(1)} %broadcast_compare_fusion.2) | copy-start | bytes 10
  8.8 47.4 %copy-start.49 = (pred[2]{0:T(512)(128)(4,1)}, pred[2]{0:T(512)(128)(4,1)S(1)}, u32[]{:S(2)}) copy-start(pred[2]{0:T(512)(128)(4,1)S(1)} %get-tuple-element.106) | copy-start | bytes 10
  20.5 7.8 %collective-permute-start.1 = (bf16[4,1,128,256]{3,2,1,0:T(8,128)(2,1)S(1)}, bf16[4,1,128,256]{3,2,1,0:T(8,128)(2,1)S(1)}, u32[]{:S(2)}, u32[]{:S(2)}) collective-permute-start(bf16[4,1,128,256]{3,2,1,0:T(8,128)(2,1)S(1)} %get-tuple-element.87), channel_id=1, source_target_pairs={{0,1},{1,2},{2,3},{3,4},{4,5},{5,6},{6,7},{8,9},{9,10},{10,11},{11... | collective-permute-start | bytes 786440 | tf_op jit(solution)/shard_map/ppermute | solution.py:21
  23.6 7.1 %collective-permute-start.2 = (bf16[4,1,128,256]{3,2,1,0:T(8,128)(2,1)S(1)}, bf16[4,1,128,256]{3,2,1,0:T(8,128)(2,1)S(1)}, u32[]{:S(2)}, u32[]{:S(2)}) collective-permute-start(bf16[4,1,128,256]{3,2,1,0:T(8,128)(2,1)S(1)} %get-tuple-element.88), channel_id=1, source_target_pairs={{1,0},{2,1},{3,2},{4,3},{5,4},{6,5},{7,6},{9,8},{10,9},{11,10},{12... | collective-permute-start | bytes 786440 | tf_op jit(solution)/shard_map/ppermute | solution.py:23
  40.3 2.2 copy-start.19
  40.3 2.8 %copy-start.20 = (bf16[2,8,128,256]{3,2,1,0:T(8,128)(2,1)S(1)}, bf16[2,8,128,256]{3,2,1,0:T(8,128)(2,1)}, u32[]{:S(2)}) copy-start(bf16[2,8,128,256]{3,2,1,0:T(8,128)(2,1)} %get-tuple-element.67) | copy-start | bytes 3145732
  40.3 3.1 %copy-start.39 = (bf16[1,1,3,256,256]{4,3,2,1,0:T(8,128)(2,1)S(1)}, bf16[1,1,3,256,256]{4,3,2,1,0:T(8,128)(2,1)}, u32[]{:S(2)}) copy-start(bf16[1,1,3,256,256]{4,3,2,1,0:T(8,128)(2,1)} %get-tuple-element.31) | copy-start | bytes 1179652
  43.4 1.5 copy-start.14
  43.4 1.9 copy-start.24
  43.4 1.9 copy-start.38
  45.3 1.5 copy-start.23
  45.3 1.6 copy-start.37
  48.3 1.3 copy-start.9
  48.3 1.5 copy-start.10
  48.3 1.6 copy-start.35
  49.9 1.5 copy-start.21
  49.9 1.6 copy-start.34
  56.2 2.4 %copy-start.1 = (bf16[2,8,128,256]{3,2,1,0:T(8,128)(2,1)S(1)}, bf16[2,8,128,256]{3,2,1,0:T(8,128)(2,1)}, u32[]{:S(2)}) copy-start(bf16[2,8,128,256]{3,2,1,0:T(8,128)(2,1)} %param.10) | copy-start | bytes 3145732
  56.2 2.4 %copy-start.4 = (f32[2,8,128,256]{3,2,1,0:T(8,128)S(1)}, f32[2,8,128,256]{3,2,1,0:T(8,128)}, u32[]{:S(2)}) copy-start(f32[2,8,128,256]{3,2,1,0:T(8,128)} %fusion.33) | copy-start | bytes 6291460
  58.5 4.2 %copy-start.46 = (f32[256]{0:T(256)S(1)}, f32[256]{0:T(256)}, u32[]{:S(2)}) copy-start(f32[256]{0:T(256)} %param.15) | copy-start | bytes 3076
  58.5 10.7 %copy-start.43 = (s32[2]{0:T(128)S(1)}, s32[2]{0:T(128)}, u32[]{:S(2)}) copy-start(s32[2]{0:T(128)} %param.11) | copy-start | bytes 28
  58.5 11.4 %copy-start.40 = (s32[3,8]{1,0:T(4,128)S(1)}, s32[3,8]{1,0:T(4,128)}, u32[]{:S(2)}) copy-start(s32[3,8]{1,0:T(4,128)} %param.12) | copy-start | bytes 292
  58.6 12.5 %copy-start.2 = (bf16[3,3,3,256,256]{4,3,2,1,0:T(8,128)(2,1)S(1)}, bf16[3,3,3,256,256]{4,3,2,1,0:T(8,128)(2,1)}, u32[]{:S(2)}) copy-start(bf16[3,3,3,256,256]{4,3,2,1,0:T(8,128)(2,1)} %param.16) | copy-start | bytes 10616836
  63.4 17.5 %collective-permute-start.3 = (bf16[2,8,128,256]{3,2,1,0:T(8,128)(2,1)S(1)}, bf16[2,8,128,256]{3,2,1,0:T(8,128)(2,1)S(1)}, u32[]{:S(2)}, u32[]{:S(2)}) collective-permute-start(bf16[2,8,128,256]{3,2,1,0:T(8,128)(2,1)S(1)} %fusion.137), channel_id=1, source_target_pairs={{0,8},{8,16},{16,24},{1,9},{9,17},{17,25},{2,10},{10,18},{18,26},{... | collective-permute-start | bytes 3145736 | tf_op jit(solution)/shard_map/ppermute | solution.py:10
  81.0 7.5 %collective-permute-start.4 = (bf16[4,1,128,256]{3,2,1,0:T(8,128)(2,1)S(1)}, bf16[4,1,128,256]{3,2,1,0:T(8,128)(2,1)S(1)}, u32[]{:S(2)}, u32[]{:S(2)}) collective-permute-start(bf16[4,1,128,256]{3,2,1,0:T(8,128)(2,1)S(1)} %get-tuple-element.83), channel_id=1, source_target_pairs={{0,1},{1,2},{2,3},{3,4},{4,5},{5,6},{6,7},{8,9},{9,10},{10,11},{11... | collective-permute-start | bytes 786440 | tf_op jit(solution)/shard_map/ppermute | solution.py:21
  85.1 7.1 %collective-permute-start.5 = (bf16[4,1,128,256]{3,2,1,0:T(8,128)(2,1)S(1)}, bf16[4,1,128,256]{3,2,1,0:T(8,128)(2,1)S(1)}, u32[]{:S(2)}, u32[]{:S(2)}) collective-permute-start(bf16[4,1,128,256]{3,2,1,0:T(8,128)(2,1)S(1)} %get-tuple-element.84), channel_id=1, source_target_pairs={{1,0},{2,1},{3,2},{4,3},{5,4},{6,5},{7,6},{9,8},{10,9},{11,10},{12... | collective-permute-start | bytes 786440 | tf_op jit(solution)/shard_map/ppermute | solution.py:23
  102.4 1.5 copy-start.18
  102.4 1.6 copy-start.33
  104.0 1.5 copy-start.16
  104.0 1.6 copy-start.32
  104.0 1.6 copy-start.50
  107.0 1.3 copy-start.30
  107.0 1.3 copy-start.52
  108.3 1.3 copy-start.29
  111.0 1.3 copy-start.6
  111.0 1.5 copy-start.7
  111.0 1.6 copy-start.27
  116.2 3.8 %copy-start.47 = (bf16[256,16]{0,1:T(8,128)(2,1)S(1)}, bf16[256,16]{0,1:T(8,128)(2,1)}, u32[]{:S(2)}) copy-start(bf16[256,16]{0,1:T(8,128)(2,1)} %param.18) | copy-start | bytes 24580
  116.2 3.8 %copy-start.48 = (f32[256]{0:T(256)S(1)}, f32[256]{0:T(256)}, u32[]{:S(2)}) copy-start(f32[256]{0:T(256)} %param.17) | copy-start | bytes 3076
  120.8 2.8 %copy-start.45 = (pred[8]{0:T(512)(128)(4,1)S(1)}, pred[8]{0:T(512)(128)(4,1)}, u32[]{:S(2)}) copy-start(pred[8]{0:T(512)(128)(4,1)} %get-tuple-element.91) | copy-start | bytes 28
  120.8 9.4 %copy-start.42 = (pred[8]{0:T(512)(128)(4,1)S(1)}, pred[8]{0:T(512)(128)(4,1)}, u32[]{:S(2)}) copy-start(pred[8]{0:T(512)(128)(4,1)} %get-tuple-element.93) | copy-start | bytes 28
  122.6 18.0 %copy-start.44 = (s32[8]{0:T(128)S(1)}, s32[8]{0:T(128)}, u32[]{:S(2)}) copy-start(s32[8]{0:T(128)} %get-tuple-element.95) | copy-start | bytes 100
  124.8 11.5 %all-to-all-start.2 = ((bf16[2,8,1,2,3072]{4,3,0,2,1:T(2,128)(2,1)}), bf16[2,8,1,2,3072]{4,3,0,2,1:T(2,128)(2,1)S(1)}, u32[]{:S(2)}, u32[]{:S(2)}) async-start(bf16[2,8,1,2,3072]{4,3,0,2,1:T(2,128)(2,1)} %copy.53), calls=%async_computation.2 | async-start | bytes 393216 | tf_op jit(solution)/shard_map/all_to_all | solution.py:135
  130.3 11.7 %copy-start.41 = (pred[8]{0:T(512)(128)(4,1)S(1)}, pred[8]{0:T(512)(128)(4,1)}, u32[]{:S(2)}) copy-start(pred[8]{0:T(512)(128)(4,1)} %get-tuple-element.92) | copy-start | bytes 28
  137.0 15.8 %all-to-all-start.1 = ((bf16[2,8,2,4,3072]{4,3,2,0,1:T(4,128)(2,1)}), bf16[2,8,2,4,3072]{4,3,2,0,1:T(4,128)(2,1)S(1)}, u32[]{:S(2)}, u32[]{:S(2)}) async-start(bf16[2,8,2,4,3072]{4,3,2,0,1:T(4,128)(2,1)} %copy.48), calls=%async_computation.1 | async-start | bytes 1572864 | tf_op jit(solution)/shard_map/all_to_all | solution.py:132
  153.8 70.2 %all-to-all-start = ((bf16[2,8,4,8,3072]{4,3,2,0,1:T(8,128)(2,1)}), bf16[2,8,4,8,3072]{4,3,2,0,1:T(8,128)(2,1)S(1)}, u32[]{:S(2)}, u32[]{:S(2)}) async-start(bf16[2,8,4,8,3072]{4,3,2,0,1:T(8,128)(2,1)} %copy.44), calls=%async_computation | async-start | bytes 6291456 | tf_op jit(solution)/shard_map/all_to_all | solution.py:129
  (14 other events, 17.2 us)
where the time goes:
time: 230 us; the launch traced here: 226 us
  waiting for transfers between devices  101 us (44%)
  local copies, waits for them, and re-layouts  43.5 us (19%)
  matrix products  35 us (15%)
  starting transfers between devices  32.3 us (14%)
  other arithmetic  13 us (6%)
    all_to_all x1, waiting for transfers between devices, body(): lax.all_to_all(embed_tokens(patch_zero, embed_weight), 'space', split_axi...  62.5 us
    dot_general x18, matrix products, causal_conv(): jnp.einsum('frwk,ko->frwo', stacked, kernel, preferred_element_type=jnp.f...  32.7 us
    ppermute x2, waiting for transfers between devices, from_behind(): return lax.ppermute(array, axis, pairs)  19.9 us
    slice x2, local copies, waits for them, and re-layouts, causal_conv(): window_rows[:, :, 0:col_count]  15.5 us
    ppermute x2, starting transfers between devices, from_behind(): return lax.ppermute(array, axis, pairs)  10.4 us
    all_to_all x1, waiting for transfers between devices, body(): lax.all_to_all(embed_tokens(patch_one, embed_weight), 'space', split_axis...  7.94 us
    unnamed x107, local copies, waits for them, and re-layouts  7.74 us
    ppermute x2, starting transfers between devices, with_halo(): lax.ppermute(tail, axis, [(i, (i + 1) % count) for i in range(ends)])  7.21 us
  transfers between devices with their start and end apart: 9, of which 7 were waited for; matrix products, arithmetic and copies ran while one was open for 9% of the time, Pallas kernels for 0%

commit v1 on v0

--- a/solution.py
+++ b/solution.py
@@ -125,17 +125,19 @@
     patch_zero = level_patches(latent, 1, band_maps[0], valid, bands)
     patch_one = level_patches(latent, 2, band_maps[1], valid, bands)
     patch_two = level_patches(latent, 4, band_maps[2], valid, bands)
-    results = [
-        lax.all_to_all(
-            embed_tokens(patch_zero, embed_weight), "space", split_axis=1, concat_axis=1, tiled=True
-        ),
-        lax.all_to_all(
-            embed_tokens(patch_one, embed_weight), "space", split_axis=1, concat_axis=1, tiled=True
-        ),
-        lax.all_to_all(
-            embed_tokens(patch_two, embed_weight), "space", split_axis=1, concat_axis=1, tiled=True
-        ),
-    ]
+    parts = (patch_zero, patch_one, patch_two)
+    flat = jnp.concatenate(
+        [p.transpose(1, 0, 2, 3, 4).reshape(bands, -1) for p in parts], axis=1
+    )
+    moved = lax.all_to_all(flat, "space", split_axis=0, concat_axis=0, tiled=True)
+    results = []
+    start = 0
+    for p in parts:
+        frames, _, rows, cols, depth = p.shape
+        size = frames * rows * cols * depth
+        piece = moved[:, start : start + size].reshape(bands, frames, rows, cols, depth)
+        start += size
+        results.append(embed_tokens(piece.transpose(1, 0, 2, 3, 4), embed_weight))
     return (settle(results[0]), settle(results[1]), settle(results[2]))
 
 

time: 230 us -> 148 us (0.64)
  the two profiles are of different devices: /device:TPU:1 before, /device:TPU:4 now
where the time goes in v1:
time: 148 us; the launch traced here: 147 us
  matrix products  36.7 us (25%)
  local copies, waits for them, and re-layouts  35.4 us (24%)
  waiting for transfers between devices  33.9 us (23%)
  starting transfers between devices  14.4 us (10%)
  other arithmetic  13.1 us (9%)
  blocking collectives  11.9 us (8%)
  between operations  1.51 us (1%)
    dot_general x18, matrix products, causal_conv(): jnp.einsum('frwk,ko->frwo', stacked, kernel, preferred_element_type=jnp.f...  32.7 us
    ppermute x2, waiting for transfers between devices, from_behind(): return lax.ppermute(array, axis, pairs)  25.3 us
    slice x2, local copies, waits for them, and re-layouts, causal_conv(): window_rows[:, :, 0:col_count]  15.5 us
    all_to_all x1, blocking collectives, body(): lax.all_to_all(flat, 'space', split_axis=0, concat_axis=0, tiled=True)  11.9 us
    ppermute x2, waiting for transfers between devices, with_halo(): lax.ppermute(head, axis, [((i + 1) % count, i) for i in range(ends)])  7.99 us
    ppermute x2, starting transfers between devices, with_halo(): lax.ppermute(tail, axis, [(i, (i + 1) % count) for i in range(ends)])  7.77 us
    unnamed x104, local copies, waits for them, and re-layouts  5.4 us
    slice x2, local copies, waits for them, and re-layouts, causal_conv(): kernel = weight[tap_time, tap_row].reshape(3 * channels, -1)  5.09 us
  transfers between devices with their start and end apart: 6, of which 5 were waited for; matrix products, arithmetic and copies ran while one was open for 6% of the time, Pallas kernels for 0%

profile of v1, /device:TPU:4, one launch (start us, length us, event | category | flops | bytes accessed | tf_op | source)
XLA Modules:
  0.0 146.8 jit_solution(11533012327307665846)
XLA Ops:
  0.6 1.6 %fusion.121 = f32[2,8,128]{2,1,0:T(8,128)S(1)} fusion(bf16[2,8,128,256]{3,2,1,0:T(8,128)(2,1)} %param.10), kind=kLoop, calls=%fused_computation.162 | loop fusion | flops 1570816 | bytes 1056768 | tf_op jit(solution)/shard_map/reduce_sum | solution.py:32
  2.3 1.9 %fusion.128 = bf16[2,8,128,256]{3,2,1,0:T(8,128)(2,1)S(1)} fusion(bf16[2,8,128,256]{3,2,1,0:T(8,128)(2,1)} %param.10, f32[256]{0:T(256)} %param.13, f32[2,8,128]{2,1,0:T(8,128)S(1)} %add_rsqrt_fusion.2), kind=kLoop, calls=%fused_computation.169 | loop fusion | flops 4194304 | bytes 2106368 | tf_op jit(solution)/shard_map/convert_element_type | solution.py:65
  4.2 1.9 %collective-permute-start = (bf16[2,8,128,256]{3,2,1,0:T(8,128)(2,1)S(1)}, bf16[2,8,128,256]{3,2,1,0:T(8,128)(2,1)S(1)}, u32[]{:S(2)}, u32[]{:S(2)}) collective-permute-start(bf16[2,8,128,256]{3,2,1,0:T(8,128)(2,1)S(1)} %fusion.128), channel_id=1, source_target_pairs={{0,8},{8,16},{16,24},{1,9},{9,17},{17,25},{2,10},{10,18},{18,26},{... | collective-permute-start | bytes 3145736 | tf_op jit(solution)/shard_map/ppermute | solution.py:10
  6.2 14.1 %collective-permute-done = bf16[2,8,128,256]{3,2,1,0:T(8,128)(2,1)S(1)} collective-permute-done((bf16[2,8,128,256]{3,2,1,0:T(8,128)(2,1)S(1)}, bf16[2,8,128,256]{3,2,1,0:T(8,128)(2,1)S(1)}, u32[]{:S(2)}, u32[]{:S(2)}) %collective-permute-start) | collective-permute-done | bytes 1048608 | tf_op jit(solution)/shard_map/ppermute | solution.py:10
  20.4 3.4 %collective-permute-start.1 = (bf16[4,1,128,256]{3,2,1,0:T(8,128)(2,1)S(1)}, bf16[4,1,128,256]{3,2,1,0:T(8,128)(2,1)S(1)}, u32[]{:S(2)}, u32[]{:S(2)}) collective-permute-start(bf16[4,1,128,256]{3,2,1,0:T(8,128)(2,1)S(1)} %get-tuple-element.90), channel_id=1, source_target_pairs={{0,1},{1,2},{2,3},{3,4},{4,5},{5,6},{6,7},{8,9},{9,10},{10,11},{11... | collective-permute-start | bytes 786440 | tf_op jit(solution)/shard_map/ppermute | solution.py:21
  23.8 1.3 collective-permute-start.2
  25.1 3.4 %fusion.213 = (bf16[1,1,3,256,256]{4,3,2,1,0:T(8,128)(2,1)S(1)}, bf16[1,1,3,256,256]{4,3,2,1,0:T(8,128)(2,1)}, bf16[1,1,3,256,256]{4,3,2,1,0:T(8,128)(2,1)}, bf1...) fusion(bf16[3,3,3,256,256]{4,3,2,1,0:T(8,128)(2,1)} %param.14), kind=kLoop, calls=%fused_computation.293 | loop fusion | bytes 7077888 | tf_op jit(solution)/shard_map/slice | solution.py:57
  28.5 3.6 %collective-permute-done.2 = bf16[4,1,128,256]{3,2,1,0:T(8,128)(2,1)S(1)} collective-permute-done((bf16[4,1,128,256]{3,2,1,0:T(8,128)(2,1)S(1)}, bf16[4,1,128,256]{3,2,1,0:T(8,128)(2,1)S(1)}, u32[]{:S(2)}, u32[]{:S(2)}) %collective-permute-start.2) | collective-permute-done | bytes 262176 | tf_op jit(solution)/shard_map/ppermute | solution.py:23
  32.0 1.2 select_maximum_fusion.3
  33.3 7.7 %fusion.215 = (bf16[2,8,128,256]{3,2,1,0:T(8,128)(2,1)S(1)}, bf16[2,8,128,256]{3,2,1,0:T(8,128)(2,1)}, bf16[2,8,128,256]{3,2,1,0:T(8,128)(2,1)}, bf16[2,8,128,25...) fusion(bf16[4,10,130,256]{3,2,1,0:T(8,128)(2,1)S(1)} %select_ma, ...), kind=kLoop, calls=%fused_computation.295 | loop fusion | bytes 37748736 | tf_op jit(solution)/shard_map/slice | solution.py:50
  41.6 2.2 %fusion.218 = (bf16[2,8,128,256]{3,2,1,0:T(8,128)(2,1)S(1)}, bf16[2,8,128,256]{3,2,1,0:T(8,128)(2,1)}, bf16[2,8,128,256]{3,2,1,0:T(8,128)(2,1)}, bf16[2,8,128,25...) fusion(bf16[4,9,128,256]{3,2,1,0:T(8,128)(2,1)S(1)} %get-tuple-element.88, ...), kind=kLoop, calls=%fused_computation.298 | loop fusion | bytes 12582912 | tf_op jit(solution)/shard_map/slice | solution.py:51
  44.7 1.3 fusion.8
  46.6 1.3 fusion.18
  48.3 1.3 fusion.23
  49.6 1.3 fusion.28
  51.2 1.3 fusion.38
  52.8 2.4 %fusion.33 = f32[2,8,128,256]{3,2,1,0:T(8,128)} fusion(bf16[768,256,1,1]{1,0,3,2:T(8,128)(2,1)S(1)} %bitcast.212, bf16[2,8,128,256]{3,2,1,0:T(8,128)(2,1)S(1)} %get-tuple-element.57, bf16[2,8,128,256]{3,2,1,0:T(8,128)(2,1)S(1)} %copy-done.20, bf16[2,8,128,256]{3,2,1,0:T(8,128)(2,1)S(1)} %copy-done.7, pred[2]{0:T(512)(128)(4,1)S(1)} %get-tuple-element.110), kind=kOutput, calls=%fused_computation.49 | convolution fusion | flops 816316416 | bytes 5636098 | tf_op jit(solution)/shard_map/frwk,ko->frwo/dot_general | solution.py:58
  55.2 2.2 %fusion.88 = f32[2,8,128,256]{3,2,1,0:T(8,128)} fusion(bf16[768,256,1,1]{1,0,3,2:T(8,128)(2,1)S(1)} %bitcast.210, bf16[2,8,128,256]{3,2,1,0:T(8,128)(2,1)S(1)} %fusion.128, bf16[2,8,128,256]{3,2,1,0:T(8,128)(2,1)S(1)} %collective-permute-done, bf16[2,8,128,256]{3,2,1,0:T(8,128)(2,1)S(1)} %get-tuple-element.61, ...), kind=kOutput, calls=%fused_computation.120 | convolution fusion | flops 819462144 | bytes 6684674 | tf_op jit(solution)/shard_map/frwk,ko->frwo/dot_general | solution.py:58
  57.5 2.4 %fusion.13 = f32[2,8,128,256]{3,2,1,0:T(8,128)} fusion(bf16[768,256,1,1]{1,0,3,2:T(8,128)(2,1)S(1)} %bitcast.208, bf16[2,8,128,256]{3,2,1,0:T(8,128)(2,1)S(1)} %get-tuple-element.67, bf16[2,8,128,256]{3,2,1,0:T(8,128)(2,1)S(1)} %collective-permute-done, bf16[2,8,128,256]{3,2,1,0:T(8,128)(2,1)S(1)} %get-tuple-element.68, pred[2]{0:T(512)(128)(4,1)S(1)} %get-tuple-element.109), kind=kOutput, calls=%fused_computation.25 | convolution fusion | flops 816316416 | bytes 5636098 | tf_op jit(solution)/shard_map/frwk,ko->frwo/dot_general | solution.py:58
  59.9 4.1 %fusion.130 = (f32[2,8,128]{2,1,0:T(8,128)S(1)}, bf16[2,8,128,256]{3,2,1,0:T(8,128)(2,1)S(1)}) fusion(bf16[768,256,1,1]{1,0,3,2:T(8,128)(2,1)S(1)} %bitcast.199, bf16[2,8,128,256]{3,2,1,0:T(8,128)(2,1)S(1)} %get-tuple-element.71, bf16[2,8,128,256]{3,2,1,0:T(8,128)(2,1)S(1)} %get-tuple-element.78, bf16[2,8,128,256]{3,2,1,0:T(8,128)(2,1)S(1)} %get-tuple-element.54, ...), kind=kOutput, calls=%fused_computation.171 | convolution fusion | flops 823654400 | bytes 22421506 | tf_op jit(solution)/shard_map/frwk,ko->frwo/dot_general | solution.py:58
  64.1 0.7 fusion.137
  64.7 1.9 %collective-permute-start.3 = (bf16[2,8,128,256]{3,2,1,0:T(8,128)(2,1)S(1)}, bf16[2,8,128,256]{3,2,1,0:T(8,128)(2,1)S(1)}, u32[]{:S(2)}, u32[]{:S(2)}) collective-permute-start(bf16[2,8,128,256]{3,2,1,0:T(8,128)(2,1)S(1)} %fusion.137), channel_id=1, source_target_pairs={{0,8},{8,16},{16,24},{1,9},{9,17},{17,25},{2,10},{10,18},{18,26},{... | collective-permute-start | bytes 3145736 | tf_op jit(solution)/shard_map/ppermute | solution.py:10
  67.9 1.7 %fusion.212 = (bf16[1,1,3,256,256]{4,3,2,1,0:T(8,128)(2,1)S(1)}, bf16[1,1,3,256,256]{4,3,2,1,0:T(8,128)(2,1)}, bf16[1,1,3,256,256]{4,3,2,1,0:T(8,128)(2,1)}, bf1...) fusion(bf16[3,3,3,256,256]{4,3,2,1,0:T(8,128)(2,1)S(1)} %copy-d, ...), kind=kLoop, calls=%fused_computation.292 | loop fusion | bytes 7077888 | tf_op jit(solution)/shard_map/slice | solution.py:57
  69.6 11.2 %collective-permute-done.3 = bf16[2,8,128,256]{3,2,1,0:T(8,128)(2,1)S(1)} collective-permute-done((bf16[2,8,128,256]{3,2,1,0:T(8,128)(2,1)S(1)}, bf16[2,8,128,256]{3,2,1,0:T(8,128)(2,1)S(1)}, u32[]{:S(2)}, u32[]{:S(2)}) %collective-permute-start.3) | collective-permute-done | bytes 1048608 | tf_op jit(solution)/shard_map/ppermute | solution.py:10
  80.9 4.4 %collective-permute-start.4 = (bf16[4,1,128,256]{3,2,1,0:T(8,128)(2,1)S(1)}, bf16[4,1,128,256]{3,2,1,0:T(8,128)(2,1)S(1)}, u32[]{:S(2)}, u32[]{:S(2)}) collective-permute-start(bf16[4,1,128,256]{3,2,1,0:T(8,128)(2,1)S(1)} %get-tuple-element.86), channel_id=1, source_target_pairs={{0,1},{1,2},{2,3},{3,4},{4,5},{5,6},{6,7},{8,9},{9,10},{10,11},{11... | collective-permute-start | bytes 786440 | tf_op jit(solution)/shard_map/ppermute | solution.py:21
  85.3 1.5 %collective-permute-start.5 = (bf16[4,1,128,256]{3,2,1,0:T(8,128)(2,1)S(1)}, bf16[4,1,128,256]{3,2,1,0:T(8,128)(2,1)S(1)}, u32[]{:S(2)}, u32[]{:S(2)}) collective-permute-start(bf16[4,1,128,256]{3,2,1,0:T(8,128)(2,1)S(1)} %get-tuple-element.87), channel_id=1, source_target_pairs={{1,0},{2,1},{3,2},{4,3},{5,4},{6,5},{7,6},{9,8},{10,9},{11,10},{12... | collective-permute-start | bytes 786440 | tf_op jit(solution)/shard_map/ppermute | solution.py:23
  86.7 1.3 fusion.171
  89.1 4.4 %collective-permute-done.5 = bf16[4,1,128,256]{3,2,1,0:T(8,128)(2,1)S(1)} collective-permute-done((bf16[4,1,128,256]{3,2,1,0:T(8,128)(2,1)S(1)}, bf16[4,1,128,256]{3,2,1,0:T(8,128)(2,1)S(1)}, u32[]{:S(2)}, u32[]{:S(2)}) %collective-permute-start.5) | collective-permute-done | bytes 262176 | tf_op jit(solution)/shard_map/ppermute | solution.py:23
  93.5 1.2 select_maximum_fusion
  94.8 7.8 %fusion.214 = (bf16[2,8,128,256]{3,2,1,0:T(8,128)(2,1)S(1)}, bf16[2,8,128,256]{3,2,1,0:T(8,128)(2,1)}, bf16[2,8,128,256]{3,2,1,0:T(8,128)(2,1)}, bf16[2,8,128,25...) fusion(bf16[4,10,130,256]{3,2,1,0:T(8,128)(2,1)S(1)} %select_ma, ...), kind=kLoop, calls=%fused_computation.294 | loop fusion | bytes 37748736 | tf_op jit(solution)/shard_map/slice | solution.py:50
  104.1 0.8 copy-done.16
  105.4 1.3 fusion.78
  107.0 1.3 fusion.48
  108.3 1.3 fusion.58
  109.6 1.3 fusion.63
  111.0 1.3 fusion.68
  112.3 1.3 fusion.73
  113.9 1.3 fusion.53
  115.3 2.2 %fusion.90 = f32[2,8,128,256]{3,2,1,0:T(8,128)} fusion(bf16[768,256,1,1]{1,0,3,2:T(8,128)(2,1)S(1)} %bitcast.202, bf16[2,8,128,256]{3,2,1,0:T(8,128)(2,1)S(1)} %fusion.137, bf16[2,8,128,256]{3,2,1,0:T(8,128)(2,1)S(1)} %collective-permute-done.3, bf16[2,8,128,256]{3,2,1,0:T(8,128)(2,1)S(1)} %get-tuple-element.43, ...), kind=kOutput, calls=%fused_computation.121 | convolution fusion | flops 819462144 | bytes 6684674 | tf_op jit(solution)/shard_map/frwk,ko->frwo/dot_general | solution.py:58
  117.5 3.8 %fusion.113 = (f32[2,8,128]{2,1,0:T(8,128)S(1)}, bf16[2,8,128,256]{3,2,1,0:T(8,128)(2,1)S(1)}) fusion(bf16[768,256,1,1]{1,0,3,2:T(8,128)(2,1)S(1)} %bitcast.198, bf16[2,8,128,256]{3,2,1,0:T(8,128)(2,1)S(1)} %get-tuple-element.53, bf16[2,8,128,256]{3,2,1,0:T(8,128)(2,1)S(1)} %get-tuple-element.72, bf16[2,8,128,256]{3,2,1,0:T(8,128)(2,1)S(1)} %get-tuple-element.36, ...), kind=kOutput, calls=%fused_computation.154 | convolution fusion | flops 823654400 | bytes 22421506 | tf_op jit(solution)/shard_map/frwk,ko->frwo/dot_general | solution.py:58
  121.3 0.8 fusion.157
  122.2 1.1 convert_bitcast_fusion
  125.3 0.7 gather_fusion.1
  126.7 0.7 gather_fusion.2
  128.9 11.9 %all_to_all.12 = bf16[8,2,2688]{2,1,0:T(2,128)(2,1)S(1)} all-to-all(bf16[8,2,2688]{2,1,0:T(2,128)(2,1)S(1)} %reshape.319), channel_id=1, replica_groups=mesh['tm'=4,'space'=8] {'space'}, dimensions={0} | all-to-all | bytes 172032 | tf_op jit(solution)/shard_map/all_to_all | solution.py:132
  141.2 2.6 %convolution_convert_fusion = bf16[2,8,4,8,3072]{4,3,2,1,0:T(8,128)(2,1)} fusion(bf16[64,3072]{1,0:T(8,128)(2,1)S(1)} %copy-done, bf16[8,2,4,8,64]{4,3,2,1,0:T(8,128)(2,1)S(1)} %reshape.265), kind=kOutput, calls=%fused_computation.6 | convolution fusion | flops 202899456 | bytes 3604480 | tf_op jit(solution)/shard_map/fbrcp,ph->fbrch/dot_general | solution.py:88
  144.2 1.5 %copy.58 = bf16[2,8,2,4,3072]{4,3,2,1,0:T(4,128)(2,1)} copy(bf16[2,8,2,4,3072]{4,1,3,2,0:T(8,128)(2,1)S(1)} %convolution_convert_fusion.1) | data formatting | bytes 1572864 | tf_op jit(solution)/shard_map/convert_element_type | solution.py:91
  146.0 0.9 copy.62
  (150 shorter events, 13.1 us)
Async XLA Ops:
  0.6 140.6 %copy-start = (bf16[64,3072]{1,0:T(8,128)(2,1)S(1)}, bf16[64,3072]{1,0:T(8,128)(2,1)}, u32[]{:S(2)}) copy-start(bf16[64,3072]{1,0:T(8,128)(2,1)} %param.19) | copy-start | bytes 1179652
  4.2 16.1 %collective-permute-start = (bf16[2,8,128,256]{3,2,1,0:T(8,128)(2,1)S(1)}, bf16[2,8,128,256]{3,2,1,0:T(8,128)(2,1)S(1)}, u32[]{:S(2)}, u32[]{:S(2)}) collective-permute-start(bf16[2,8,128,256]{3,2,1,0:T(8,128)(2,1)S(1)} %fusion.128), channel_id=1, source_target_pairs={{0,8},{8,16},{16,24},{1,9},{9,17},{17,25},{2,10},{10,18},{18,26},{... | collective-permute-start | bytes 3145736 | tf_op jit(solution)/shard_map/ppermute | solution.py:10
  6.1 49.1 %copy-start.48 = (pred[2]{0:T(512)(128)(4,1)}, pred[2]{0:T(512)(128)(4,1)S(1)}, u32[]{:S(2)}) copy-start(pred[2]{0:T(512)(128)(4,1)S(1)} %broadcast_compare_fusion.2) | copy-start | bytes 10
  6.2 51.3 %copy-start.46 = (pred[2]{0:T(512)(128)(4,1)}, pred[2]{0:T(512)(128)(4,1)S(1)}, u32[]{:S(2)}) copy-start(pred[2]{0:T(512)(128)(4,1)S(1)} %get-tuple-element.109) | copy-start | bytes 10
  20.4 8.1 %collective-permute-start.1 = (bf16[4,1,128,256]{3,2,1,0:T(8,128)(2,1)S(1)}, bf16[4,1,128,256]{3,2,1,0:T(8,128)(2,1)S(1)}, u32[]{:S(2)}, u32[]{:S(2)}) collective-permute-start(bf16[4,1,128,256]{3,2,1,0:T(8,128)(2,1)S(1)} %get-tuple-element.90), channel_id=1, source_target_pairs={{0,1},{1,2},{2,3},{3,4},{4,5},{5,6},{6,7},{8,9},{9,10},{10,11},{11... | collective-permute-start | bytes 786440 | tf_op jit(solution)/shard_map/ppermute | solution.py:21
  23.8 8.3 %collective-permute-start.2 = (bf16[4,1,128,256]{3,2,1,0:T(8,128)(2,1)S(1)}, bf16[4,1,128,256]{3,2,1,0:T(8,128)(2,1)S(1)}, u32[]{:S(2)}, u32[]{:S(2)}) collective-permute-start(bf16[4,1,128,256]{3,2,1,0:T(8,128)(2,1)S(1)} %get-tuple-element.91), channel_id=1, source_target_pairs={{1,0},{2,1},{3,2},{4,3},{5,4},{6,5},{7,6},{9,8},{10,9},{11,10},{12... | collective-permute-start | bytes 786440 | tf_op jit(solution)/shard_map/ppermute | solution.py:23
  41.6 2.2 %copy-start.18 = (bf16[2,8,128,256]{3,2,1,0:T(8,128)(2,1)S(1)}, bf16[2,8,128,256]{3,2,1,0:T(8,128)(2,1)}, u32[]{:S(2)}) copy-start(bf16[2,8,128,256]{3,2,1,0:T(8,128)(2,1)} %get-tuple-element.69) | copy-start | bytes 3145732
  41.6 2.8 %copy-start.19 = (bf16[2,8,128,256]{3,2,1,0:T(8,128)(2,1)S(1)}, bf16[2,8,128,256]{3,2,1,0:T(8,128)(2,1)}, u32[]{:S(2)}) copy-start(bf16[2,8,128,256]{3,2,1,0:T(8,128)(2,1)} %get-tuple-element.70) | copy-start | bytes 3145732
  41.6 3.1 %copy-start.37 = (bf16[1,1,3,256,256]{4,3,2,1,0:T(8,128)(2,1)S(1)}, bf16[1,1,3,256,256]{4,3,2,1,0:T(8,128)(2,1)}, u32[]{:S(2)}) copy-start(bf16[1,1,3,256,256]{4,3,2,1,0:T(8,128)(2,1)} %get-tuple-element.34) | copy-start | bytes 1179652
  44.7 1.3 copy-start.12
  44.7 1.5 %copy-start.13 = (bf16[2,8,128,256]{3,2,1,0:T(8,128)(2,1)S(1)}, bf16[2,8,128,256]{3,2,1,0:T(8,128)(2,1)}, u32[]{:S(2)}) copy-start(bf16[2,8,128,256]{3,2,1,0:T(8,128)(2,1)} %get-tuple-element.66) | copy-start | bytes 3145732
  44.7 1.9 %copy-start.23 = (bf16[2,8,128,256]{3,2,1,0:T(8,128)(2,1)S(1)}, bf16[2,8,128,256]{3,2,1,0:T(8,128)(2,1)}, u32[]{:S(2)}) copy-start(bf16[2,8,128,256]{3,2,1,0:T(8,128)(2,1)} %get-tuple-element.80) | copy-start | bytes 3145732
  44.7 1.9 %copy-start.36 = (bf16[1,1,3,256,256]{4,3,2,1,0:T(8,128)(2,1)S(1)}, bf16[1,1,3,256,256]{4,3,2,1,0:T(8,128)(2,1)}, u32[]{:S(2)}) copy-start(bf16[1,1,3,256,256]{4,3,2,1,0:T(8,128)(2,1)} %get-tuple-element.32) | copy-start | bytes 1179652
  46.6 1.5 %copy-start.22 = (bf16[2,8,128,256]{3,2,1,0:T(8,128)(2,1)S(1)}, bf16[2,8,128,256]{3,2,1,0:T(8,128)(2,1)}, u32[]{:S(2)}) copy-start(bf16[2,8,128,256]{3,2,1,0:T(8,128)(2,1)} %get-tuple-element.106) | copy-start | bytes 3145732
  46.6 1.6 %copy-start.35 = (bf16[1,1,3,256,256]{4,3,2,1,0:T(8,128)(2,1)S(1)}, bf16[1,1,3,256,256]{4,3,2,1,0:T(8,128)(2,1)}, u32[]{:S(2)}) copy-start(bf16[1,1,3,256,256]{4,3,2,1,0:T(8,128)(2,1)} %get-tuple-element.31) | copy-start | bytes 1179652
  49.6 1.3 copy-start.8
  49.6 1.5 %copy-start.9 = (bf16[2,8,128,256]{3,2,1,0:T(8,128)(2,1)S(1)}, bf16[2,8,128,256]{3,2,1,0:T(8,128)(2,1)}, u32[]{:S(2)}) copy-start(bf16[2,8,128,256]{3,2,1,0:T(8,128)(2,1)} %get-tuple-element.56) | copy-start | bytes 3145732
  49.6 1.6 %copy-start.33 = (bf16[1,1,3,256,256]{4,3,2,1,0:T(8,128)(2,1)S(1)}, bf16[1,1,3,256,256]{4,3,2,1,0:T(8,128)(2,1)}, u32[]{:S(2)}) copy-start(bf16[1,1,3,256,256]{4,3,2,1,0:T(8,128)(2,1)} %get-tuple-element.35) | copy-start | bytes 1179652
  51.2 1.5 %copy-start.20 = (bf16[2,8,128,256]{3,2,1,0:T(8,128)(2,1)S(1)}, bf16[2,8,128,256]{3,2,1,0:T(8,128)(2,1)}, u32[]{:S(2)}) copy-start(bf16[2,8,128,256]{3,2,1,0:T(8,128)(2,1)} %get-tuple-element.107) | copy-start | bytes 3145732
  51.2 1.6 %copy-start.32 = (bf16[1,1,3,256,256]{4,3,2,1,0:T(8,128)(2,1)S(1)}, bf16[1,1,3,256,256]{4,3,2,1,0:T(8,128)(2,1)}, u32[]{:S(2)}) copy-start(bf16[1,1,3,256,256]{4,3,2,1,0:T(8,128)(2,1)} %get-tuple-element.28) | copy-start | bytes 1179652
  57.4 2.4 %copy-start.1 = (bf16[2,8,128,256]{3,2,1,0:T(8,128)(2,1)S(1)}, bf16[2,8,128,256]{3,2,1,0:T(8,128)(2,1)}, u32[]{:S(2)}) copy-start(bf16[2,8,128,256]{3,2,1,0:T(8,128)(2,1)} %param.10) | copy-start | bytes 3145732
  57.4 2.4 %copy-start.3 = (f32[2,8,128,256]{3,2,1,0:T(8,128)S(1)}, f32[2,8,128,256]{3,2,1,0:T(8,128)}, u32[]{:S(2)}) copy-start(f32[2,8,128,256]{3,2,1,0:T(8,128)} %fusion.33) | copy-start | bytes 6291460
  59.8 4.2 %copy-start.43 = (f32[256]{0:T(256)S(1)}, f32[256]{0:T(256)}, u32[]{:S(2)}) copy-start(f32[256]{0:T(256)} %param.15) | copy-start | bytes 3076
  59.8 6.8 %copy-start.38 = (s32[3,8]{1,0:T(4,128)S(1)}, s32[3,8]{1,0:T(4,128)}, u32[]{:S(2)}) copy-start(s32[3,8]{1,0:T(4,128)} %param.12) | copy-start | bytes 292
  59.9 6.8 %copy-start.41 = (s32[2]{0:T(128)S(1)}, s32[2]{0:T(128)}, u32[]{:S(2)}) copy-start(s32[2]{0:T(128)} %param.11) | copy-start | bytes 28
  59.9 8.1 %copy-start.2 = (bf16[3,3,3,256,256]{4,3,2,1,0:T(8,128)(2,1)S(1)}, bf16[3,3,3,256,256]{4,3,2,1,0:T(8,128)(2,1)}, u32[]{:S(2)}) copy-start(bf16[3,3,3,256,256]{4,3,2,1,0:T(8,128)(2,1)} %param.16) | copy-start | bytes 10616836
  64.7 16.1 %collective-permute-start.3 = (bf16[2,8,128,256]{3,2,1,0:T(8,128)(2,1)S(1)}, bf16[2,8,128,256]{3,2,1,0:T(8,128)(2,1)S(1)}, u32[]{:S(2)}, u32[]{:S(2)}) collective-permute-start(bf16[2,8,128,256]{3,2,1,0:T(8,128)(2,1)S(1)} %fusion.137), channel_id=1, source_target_pairs={{0,8},{8,16},{16,24},{1,9},{9,17},{17,25},{2,10},{10,18},{18,26},{... | collective-permute-start | bytes 3145736 | tf_op jit(solution)/shard_map/ppermute | solution.py:10
  80.9 8.2 %collective-permute-start.4 = (bf16[4,1,128,256]{3,2,1,0:T(8,128)(2,1)S(1)}, bf16[4,1,128,256]{3,2,1,0:T(8,128)(2,1)S(1)}, u32[]{:S(2)}, u32[]{:S(2)}) collective-permute-start(bf16[4,1,128,256]{3,2,1,0:T(8,128)(2,1)S(1)} %get-tuple-element.86), channel_id=1, source_target_pairs={{0,1},{1,2},{2,3},{3,4},{4,5},{5,6},{6,7},{8,9},{9,10},{10,11},{11... | collective-permute-start | bytes 786440 | tf_op jit(solution)/shard_map/ppermute | solution.py:21
  85.3 8.3 %collective-permute-start.5 = (bf16[4,1,128,256]{3,2,1,0:T(8,128)(2,1)S(1)}, bf16[4,1,128,256]{3,2,1,0:T(8,128)(2,1)S(1)}, u32[]{:S(2)}, u32[]{:S(2)}) collective-permute-start(bf16[4,1,128,256]{3,2,1,0:T(8,128)(2,1)S(1)} %get-tuple-element.87), channel_id=1, source_target_pairs={{1,0},{2,1},{3,2},{4,3},{5,4},{6,5},{7,6},{9,8},{10,9},{11,10},{12... | collective-permute-start | bytes 786440 | tf_op jit(solution)/shard_map/ppermute | solution.py:23
  103.7 1.5 %copy-start.17 = (bf16[2,8,128,256]{3,2,1,0:T(8,128)(2,1)S(1)}, bf16[2,8,128,256]{3,2,1,0:T(8,128)(2,1)}, u32[]{:S(2)}) copy-start(bf16[2,8,128,256]{3,2,1,0:T(8,128)(2,1)} %get-tuple-element.38) | copy-start | bytes 3145732
  103.7 1.6 %copy-start.31 = (bf16[1,1,3,256,256]{4,3,2,1,0:T(8,128)(2,1)S(1)}, bf16[1,1,3,256,256]{4,3,2,1,0:T(8,128)(2,1)}, u32[]{:S(2)}) copy-start(bf16[1,1,3,256,256]{4,3,2,1,0:T(8,128)(2,1)} %get-tuple-element.26) | copy-start | bytes 1179652
  105.3 1.3 copy-start.14
  105.3 1.5 %copy-start.15 = (bf16[2,8,128,256]{3,2,1,0:T(8,128)(2,1)S(1)}, bf16[2,8,128,256]{3,2,1,0:T(8,128)(2,1)}, u32[]{:S(2)}) copy-start(bf16[2,8,128,256]{3,2,1,0:T(8,128)(2,1)} %get-tuple-element.52) | copy-start | bytes 3145732
  105.3 1.6 %copy-start.30 = (bf16[1,1,3,256,256]{4,3,2,1,0:T(8,128)(2,1)S(1)}, bf16[1,1,3,256,256]{4,3,2,1,0:T(8,128)(2,1)}, u32[]{:S(2)}) copy-start(bf16[1,1,3,256,256]{4,3,2,1,0:T(8,128)(2,1)} %get-tuple-element.25) | copy-start | bytes 1179652
  105.4 1.6 %copy-start.47 = (pred[2]{0:T(512)(128)(4,1)S(1)}, pred[2]{0:T(512)(128)(4,1)}, u32[]{:S(2)}) copy-start(pred[2]{0:T(512)(128)(4,1)} %copy-done.46) | copy-start | bytes 10
  108.3 1.3 copy-start.28
  108.3 1.3 copy-start.49
  109.6 1.3 copy-start.27
  111.0 1.3 copy-start.26
  112.3 1.3 copy-start.5
  112.3 1.5 %copy-start.6 = (bf16[2,8,128,256]{3,2,1,0:T(8,128)(2,1)S(1)}, bf16[2,8,128,256]{3,2,1,0:T(8,128)(2,1)}, u32[]{:S(2)}) copy-start(bf16[2,8,128,256]{3,2,1,0:T(8,128)(2,1)} %get-tuple-element.50) | copy-start | bytes 3145732
  112.3 1.6 %copy-start.25 = (bf16[1,1,3,256,256]{4,3,2,1,0:T(8,128)(2,1)S(1)}, bf16[1,1,3,256,256]{4,3,2,1,0:T(8,128)(2,1)}, u32[]{:S(2)}) copy-start(bf16[1,1,3,256,256]{4,3,2,1,0:T(8,128)(2,1)} %get-tuple-element.24) | copy-start | bytes 1179652
  113.9 1.3 copy-start.24
  117.5 3.8 %copy-start.44 = (bf16[256,16]{0,1:T(8,128)(2,1)S(1)}, bf16[256,16]{0,1:T(8,128)(2,1)}, u32[]{:S(2)}) copy-start(bf16[256,16]{0,1:T(8,128)(2,1)} %param.18) | copy-start | bytes 24580
  117.5 3.8 %copy-start.45 = (f32[256]{0:T(256)S(1)}, f32[256]{0:T(256)}, u32[]{:S(2)}) copy-start(f32[256]{0:T(256)} %param.17) | copy-start | bytes 3076
  122.1 2.5 %copy-start.40 = (pred[8]{0:T(512)(128)(4,1)S(1)}, pred[8]{0:T(512)(128)(4,1)}, u32[]{:S(2)}) copy-start(pred[8]{0:T(512)(128)(4,1)} %get-tuple-element.94) | copy-start | bytes 28
  122.1 3.9 %copy-start.39 = (pred[8]{0:T(512)(128)(4,1)S(1)}, pred[8]{0:T(512)(128)(4,1)}, u32[]{:S(2)}) copy-start(pred[8]{0:T(512)(128)(4,1)} %get-tuple-element.96) | copy-start | bytes 28
  122.1 5.3 %copy-start.42 = (pred[8]{0:T(512)(128)(4,1)S(1)}, pred[8]{0:T(512)(128)(4,1)}, u32[]{:S(2)}) copy-start(pred[8]{0:T(512)(128)(4,1)} %get-tuple-element.95) | copy-start | bytes 28
  (8 other events, 10.3 us)

commit v2 on v1

v2 whole, which is shorter than its diff:
```python
import functools

import jax
import jax.numpy as jnp
from jax import lax
from jax.experimental import pallas as pl
from jax.experimental.pallas import tpu as pltpu
from jax.sharding import PartitionSpec as P

MESH = pl.DeviceIdType.MESH
ROW_BLOCK = 2


def activate(values, gain_row):
    meansq = jnp.mean(values * values, axis=-1, keepdims=True)
    half = values * lax.rsqrt(meansq + 1e-06) * (gain_row * 0.5)
    return half + half * jnp.tanh(half)


def encoder_kernel(
    clip_len,
    bands,
    clip_ref,
    maps_ref,
    x_ref,
    gains_ref,
    lat_ref,
    w1_hbm,
    w2_hbm,
    out_ref,
    w_one,
    w_two,
    ext_one,
    ext_two,
    mid_stream,
    lat_rows,
    fine_rows,
    mid_rows,
    coarse_rows,
    pool_mid,
    pool_coarse,
    fine_bands,
    mid_bands,
    coarse_bands,
    stage,
    send_buf,
    recv_buf,
    w_sem,
    halo_send,
    halo_recv,
    band_send,
    band_recv,
):
    frames, rows, cols, chans = x_ref.shape
    time = lax.axis_index("tm")
    place = lax.axis_index("space")
    first = time * frames
    has_prev = lax.rem(first, clip_len) != 0
    has_next = lax.rem(first + frames, clip_len) != 0
    has_up = place > 0
    has_down = place < bands - 1

    weight_copies = [
        [
            pltpu.make_async_copy(src.at[:, kx], dst.at[kx], w_sem.at[sec, kx])
            for kx in range(3)
        ]
        for sec, (src, dst) in enumerate(((w1_hbm, w_one), (w2_hbm, w_two)))
    ]
    for group in weight_copies:
        for copy in group:
            copy.start()

    barrier = pltpu.get_barrier_semaphore()
    links = [
        (has_next, time + 1, place),
        (has_prev, time - 1, place),
        (has_next & has_up, time + 1, place - 1),
        (has_next & has_down, time + 1, place + 1),
        (has_prev & has_up, time - 1, place - 1),
        (has_prev & has_down, time - 1, place + 1),
    ]
    for there, t, s in links:

        @pl.when(there)
        def _():
            pl.semaphore_signal(
                barrier, inc=1, device_id={"tm": t, "space": s}, device_id_type=MESH
            )

    for step in range(1, bands):
        pl.semaphore_signal(
            barrier,
            inc=1,
            device_id={"tm": time, "space": lax.rem(place + step, bands)},
            device_id_type=MESH,
        )

    gain_one = gains_ref[0:1, :]
    gain_two = gains_ref[1:2, :]
    gain_out = gains_ref[2:3, :]

    for ext in (ext_one, ext_two):

        @pl.when(jnp.logical_not(has_prev))
        def _():
            ext[0:2] = jnp.zeros((2, rows + 2, cols, chans), jnp.bfloat16)

        @pl.when(jnp.logical_not(has_up))
        def _():
            ext[:, 0] = jnp.zeros((frames + 2, cols, chans), jnp.bfloat16)

        @pl.when(jnp.logical_not(has_down))
        def _():
            ext[:, rows + 1] = jnp.zeros((frames + 2, cols, chans), jnp.bfloat16)

    @pl.loop(0, rows)
    def _(r):
        for f in range(frames):
            values = x_ref[f, r].astype(jnp.float32)
            ext_one[2 + f, r + 1] = activate(values, gain_one).astype(jnp.bfloat16)

    peers = bands - 1
    for there, _, _ in links:
        peers = peers + jnp.where(there, 1, 0)
    pl.semaphore_wait(barrier, peers)

    def halo(sec, ext):
        sends = (
            (has_next, ext.at[frames : frames + 2, 1 : rows + 1], ext.at[0:2, 1 : rows + 1], 1, 0),
            (has_up, ext.at[2 : frames + 2, 1], ext.at[2 : frames + 2, rows + 1], 0, -1),
            (has_down, ext.at[2 : frames + 2, rows], ext.at[2 : frames + 2, 0], 0, 1),
            (has_next & has_up, ext.at[frames : frames + 2, 1], ext.at[0:2, rows + 1], 1, -1),
            (has_next & has_down, ext.at[frames : frames + 2, rows], ext.at[0:2, 0], 1, 1),
        )
        waits = (has_prev, has_down, has_up, has_prev & has_down, has_prev & has_up)
        made = []
        for k, (there, src, dst, dt, ds) in enumerate(sends):
            copy = pltpu.make_async_remote_copy(
                src_ref=src,
                dst_ref=dst,
                send_sem=halo_send.at[sec, k],
                recv_sem=halo_recv.at[sec, k],
                device_id={"tm": time + dt, "space": place + ds},
                device_id_type=MESH,
            )
            made.append((there, waits[k], copy))
        return made

    def start_all(made):
        for k in (1, 2, 3, 4, 0):
            there, _, copy = made[k]

            @pl.when(there)
            def _():
                copy.start()

    def finish_recv(made):
        for _, here, copy in made:

            @pl.when(here)
            def _():
                copy.wait_recv()

    def finish_send(made):
        for there, _, copy in made:

            @pl.when(there)
            def _():
                copy.wait_send()

    col_id = lax.broadcasted_iota(jnp.int32, (cols, chans), 0)
    size = ROW_BLOCK * cols

    def conv_rows(ext, weight, r0, f):
        lhs = jnp.concatenate(
            [
                ext[f + kt, pl.ds(r0 + ky, ROW_BLOCK)].reshape(size, chans)
                for kt in range(3)
                for ky in range(3)
            ],
            axis=1,
        )
        taps = [
            jnp.dot(
                lhs,
                weight[kx].reshape(9 * chans, chans),
                preferred_element_type=jnp.float32,
            )
            for kx in range(3)
        ]
        done = []
        for k in range(ROW_BLOCK):
            left, mid, right = (tap[k * cols : (k + 1) * cols] for tap in taps)
            left = jnp.where(col_id == 0, 0.0, pltpu.roll(left, 1, 0))
            right = jnp.where(col_id == cols - 1, 0.0, pltpu.roll(right, cols - 1, 0))
            done.append(mid + left + right)
        return done

    halo_one = halo(0, ext_one)
    start_all(halo_one)
    for copy in weight_copies[0]:
        copy.wait()
    finish_recv(halo_one)

    @pl.loop(0, rows // ROW_BLOCK)
    def _(block):
        r0 = block * ROW_BLOCK
        for f in range(frames):
            for k, update in enumerate(conv_rows(ext_one, w_one, r0, f)):
                total = x_ref[f, r0 + k].astype(jnp.float32) + update
                rounded = total.astype(jnp.bfloat16)
                mid_stream[f, r0 + k] = rounded
                ext_two[2 + f, r0 + k + 1] = activate(
                    rounded.astype(jnp.float32), gain_two
                ).astype(jnp.bfloat16)

    halo_two = halo(1, ext_two)
    start_all(halo_two)
    for copy in weight_copies[1]:
        copy.wait()
    finish_recv(halo_two)

    @pl.loop(0, rows // ROW_BLOCK)
    def _(block):
        r0 = block * ROW_BLOCK
        latents = [jnp.zeros((cols, 128), jnp.float32)] * ROW_BLOCK
        for f in range(frames):
            for k, update in enumerate(conv_rows(ext_two, w_two, r0, f)):
                total = mid_stream[f, r0 + k].astype(jnp.float32) + update
                final = activate(
                    total.astype(jnp.bfloat16).astype(jnp.float32), gain_out
                ).astype(jnp.bfloat16)
                latents[k] = latents[k] + jnp.dot(
                    final, lat_ref[f], preferred_element_type=jnp.float32
                )
        for k in range(ROW_BLOCK):
            lat_rows[r0 + k] = latents[k]

    finish_send(halo_one)
    finish_send(halo_two)

    clip = lax.div(first, clip_len)
    limit = clip_ref[clip]

    def pyramid(source, count, width, patch_rows, pooled):
        lane = lax.broadcasted_iota(jnp.int32, (width, 128), 1)
        group = lax.rem(lax.div(lane, 16), 4)
        position = first - clip * clip_len + lax.div(lane, 64)
        keep = position < limit
        for i in range(count):
            total = None
            chosen = None
            for p in range(2):
                for q in range(2):
                    part = source[2 * i + p, pl.ds(q, width, stride=2), :]
                    total = part if total is None else total + part
                    chosen = (
                        part
                        if chosen is None
                        else jnp.where(group == 2 * p + q, part, chosen)
                    )
            patch_rows[i] = jnp.where(keep, chosen, 0.0)
            if pooled is not None:
                pooled[i] = total * 0.25

    levels = (
        (lat_rows, fine_rows, pool_mid, fine_bands),
        (pool_mid, mid_rows, pool_coarse, mid_bands),
        (pool_coarse, coarse_rows, None, coarse_bands),
    )
    stage[...] = jnp.zeros_like(stage)
    offset = 0
    for level, (source, patch_rows, pooled, by_band) in enumerate(levels):
        count, width, _ = patch_rows.shape
        pyramid(source, count, width, patch_rows, pooled)
        each = width // bands
        for b in range(bands):
            for i in range(count):
                by_band[b, i * each : (i + 1) * each] = patch_rows[
                    i, b * each : (b + 1) * each
                ]
        for d in range(bands):
            stage[d, offset : offset + count * each] = by_band[maps_ref[level, d]]
        offset += count * each
    for d in range(bands):
        send_buf[d] = stage[d].astype(jnp.bfloat16)

    moves = []
    for step in range(1, bands):
        target = lax.rem(place + step, bands)
        copy = pltpu.make_async_remote_copy(
            src_ref=send_buf.at[target],
            dst_ref=recv_buf.at[place],
            send_sem=band_send.at[step - 1],
            recv_sem=band_recv.at[step - 1],
            device_id={"tm": time, "space": target},
            device_id_type=MESH,
        )
        copy.start()
        moves.append(copy)
    recv_buf[place] = send_buf[place]
    for copy in moves:
        copy.wait_recv()
    for copy in moves:
        copy.wait_send()
    out_ref[...] = recv_buf[...]


def encode(features, clip_frames, band_maps, gains, latents, conv_one, conv_two, clip_len):
    bands = lax.axis_size("space")
    frames, rows, cols, chans = features.shape
    counts = [
        (rows // s // 2, cols // s // 2) for s in (1, 2, 4)
    ]
    used = sum(n * w // bands for n, w in counts)
    message = -(-used // 16) * 16
    f32, bf16 = jnp.float32, jnp.bfloat16
    vmem = pl.BlockSpec(memory_space=pltpu.VMEM)
    smem = pl.BlockSpec(memory_space=pltpu.SMEM)
    hbm = pl.BlockSpec(memory_space=pl.ANY)
    weight = pltpu.VMEM((3, 9, chans, chans), bf16)
    ext = pltpu.VMEM((frames + 2, rows + 2, cols, chans), bf16)
    scratch = [weight, weight, ext, ext, pltpu.VMEM((frames, rows, cols, chans), bf16)]
    scratch.append(pltpu.VMEM((rows, cols, 128), f32))
    scratch += [pltpu.VMEM((n, w, 128), f32) for n, w in counts]
    scratch += [pltpu.VMEM((n, w, 128), f32) for n, w in counts[:2]]
    scratch += [pltpu.VMEM((bands, n * w // bands, 128), f32) for n, w in counts]
    scratch += [
        pltpu.VMEM((bands, message, 128), f32),
        pltpu.VMEM((bands, message, 128), bf16),
        pltpu.VMEM((bands, message, 128), bf16),
        pltpu.SemaphoreType.DMA((2, 3)),
        pltpu.SemaphoreType.DMA((2, 5)),
        pltpu.SemaphoreType.DMA((2, 5)),
        pltpu.SemaphoreType.DMA((bands - 1,)),
        pltpu.SemaphoreType.DMA((bands - 1,)),
    ]
    return pl.pallas_call(
        functools.partial(encoder_kernel, clip_len, bands),
        out_shape=jax.ShapeDtypeStruct((bands, message, 128), bf16),
        in_specs=[smem, smem, vmem, vmem, vmem, hbm, hbm],
        out_specs=vmem,
        scratch_shapes=scratch,
        compiler_params=pltpu.CompilerParams(
            collective_id=0, has_side_effects=True, vmem_limit_bytes=52 * 1024 * 1024
        ),
        name="encoder",
    )(clip_frames, band_maps, features, gains, latents, conv_one, conv_two)


def body(
    features,
    clip_frames,
    band_maps,
    gain_one,
    conv_one,
    gain_two,
    conv_two,
    gain_out,
    latent_weight,
    embed_weight,
):
    frames, rows, cols, chans = features.shape
    clip_len = frames * lax.axis_size("tm") // 2
    bands = lax.axis_size("space")
    gains = jnp.stack([gain_one, gain_two, gain_out])
    repeated = jnp.tile(latent_weight, (1, 4))
    blank = jnp.zeros_like(repeated)
    latents = jnp.stack(
        [
            jnp.concatenate([repeated, blank], axis=1),
            jnp.concatenate([blank, repeated], axis=1),
        ]
    )
    moved = encode(
        features,
        clip_frames,
        band_maps,
        gains,
        latents,
        conv_one.reshape(9, 3, chans, chans),
        conv_two.reshape(9, 3, chans, chans),
        clip_len,
    )
    depth = embed_weight.shape[0]
    results = []
    start = 0
    for s in (1, 2, 4):
        count, each = rows // s // 2, cols // s // 2 // bands
        piece = moved[:, start : start + count * each]
        start += count * each
        piece = piece.reshape(bands * count, each, frames, depth).transpose(2, 0, 1, 3)
        embedded = jnp.einsum(
            "fice,eh->fich", piece, embed_weight, preferred_element_type=jnp.float32
        ).astype(jnp.bfloat16)
        results.append(embedded[:, None])
    return tuple(results)


def solution(mesh):
    return jax.shard_map(
        body,
        mesh=mesh,
        in_specs=(P("tm", "space", None, None), P(), P(), P(), P(), P(), P(), P(), P(), P()),
        out_specs=(
            P("tm", "space", None, None, None),
            P("tm", "space", None, None, None),
            P("tm", "space", None, None, None),
        ),
        check_vma=False,
    )
```

time: 148 us -> 56.6 us (0.38)
  the two profiles are of different devices: /device:TPU:4 before, /device:TPU:1 now
where the time goes in v2:
time: 56.6 us; the launch traced here: 56.3 us
  Pallas kernels  45.5 us (80%)
  local copies, waits for them, and re-layouts  6.12 us (11%)
  matrix products  3.16 us (6%)
  other arithmetic  0.79 us (1%)
  between operations  0.72 us (1%)
    pallas_call x1, Pallas kernels, encode(): pl.pallas_call(functools.partial(encoder_kernel, clip_len, bands), out_sh...  45.5 us
    unnamed x10, local copies, waits for them, and re-layouts  4.93 us
    dot_general x3, matrix products, body(): jnp.einsum('fice,eh->fich', piece, embed_weight, preferred_element_type=j...  3.16 us

profile of v2, /device:TPU:1, one launch (start us, length us, event | category | flops | bytes accessed | tf_op | source)
XLA Modules:
  0.0 56.3 jit_solution(7365259563991610939)
XLA Ops:
  0.6 0.0 copy-start
  0.6 0.8 %pad_maximum_fusion.1.gains_ref = f32[3,256]{1,0:T(4,128)S(1)} fusion(f32[1,256]{1,0:T(1,128)} %bitcast.39, f32[1,256]{1,0:T(1,128)} %bitcast.40, f32[1,256]{1,0:T(1,128)} %bitcast.41), kind=kLoop, calls=%fused_computation.18 | loop fusion | flops 1536 | bytes 6144 | tf_op jit(solution)/shard_map/stack | solution.py:367
  1.4 0.7 %tile.4 = bf16[256,4,16]{0,2,1:T(8,128)(2,1)S(1)} broadcast(bf16[256,16]{0,1:T(8,128)(2,1)} %param.18), dimensions={0,2} | broadcast | bytes 40960 | tf_op jit(solution)/shard_map/tile | solution.py:368
  2.1 0.1 copy.20
  2.2 0.1 pad_bitcast_fusion.1
  2.4 0.0 copy-start.1
  2.4 1.2 %copy-done.1 = bf16[2,8,128,256]{3,2,1,0:T(8,128)(2,1)S(1)} copy-done((bf16[2,8,128,256]{3,2,1,0:T(8,128)(2,1)S(1)}, bf16[2,8,128,256]{3,2,1,0:T(8,128)(2,1)}, u32[]{:S(2)}) %copy-start.1) | copy-done | bytes 1048600
  3.6 0.0 copy-start.2
  3.6 0.7 %copy-done.2 = s32[3,8]{1,0:T(4,128)S(1)} copy-done((s32[3,8]{1,0:T(4,128)S(1)}, s32[3,8]{1,0:T(4,128)}, u32[]{:S(2)}) %copy-start.2) | copy-done | bytes 120
  4.3 0.0 copy-start.3
  4.3 0.7 %copy-done.3 = s32[2]{0:T(128)S(1)} copy-done((s32[2]{0:T(128)S(1)}, s32[2]{0:T(128)}, u32[]{:S(2)}) %copy-start.3) | copy-done | bytes 32
  4.9 45.5 %encoder.1 = bf16[8,48,128]{2,1,0:T(8,128)(2,1)S(1)} custom-call(s32[2]{0:T(128)S(1)} %copy-done.3, s32[3,8]{1,0:T(4,128)S(1)} %copy-done.2, bf16[2,8,128,256]{3,2,1,0:T(8,128)(2,1)S(1)} %copy-done.1, f32[3,256]{1,0:T(4,128)S(1)} %pad_maximum_fusion.1.gains_ref, bf16[2,256,128]{2,1,0:T(8,128)(2,1)S(1)} %pad_maximum_fusion.lat_ref, ...), custom_call_target="tpu_custom_call" | custom-call | tf_op jit(solution)/shard_map/encoder/pallas_call | solution.py:339
  50.4 0.1 reshape.29
  50.5 0.1 reshape.28
  50.6 0.1 reshape.27
  50.7 0.0 copy-done
  50.7 0.2 fusion.2
  50.9 0.9 %copy.27 = bf16[2,1,8,2,3072]{4,3,2,1,0:T(2,128)(2,1)} copy(bf16[2,1,8,2,3072]{4,2,3,0,1:T(8,128)(2,1)S(1)} %fusion.2) | data formatting | bytes 393216
  51.8 0.3 fusion.1
  52.2 1.5 %copy.26 = bf16[2,1,16,4,3072]{4,3,2,1,0:T(4,128)(2,1)} copy(bf16[2,1,16,4,3072]{4,2,3,0,1:T(8,128)(2,1)S(1)} %fusion.1) | data formatting | bytes 1572864
  53.7 2.6 %fusion = bf16[2,1,32,8,3072]{4,3,2,1,0:T(8,128)(2,1)} fusion(bf16[64,3072]{1,0:T(8,128)(2,1)S(1)} %copy-done, bf16[32,8,2,64]{3,2,1,0:T(2,128)(2,1)S(1)} %reshape.27), kind=kOutput, calls=%fused_computation.1 | convolution fusion | flops 202899456 | bytes 3604480 | tf_op jit(solution)/shard_map/fice,eh->fich/dot_general | solution.py:394
  (4 shorter events, 0.0 us)
Async XLA Ops:
  0.6 50.1 %copy-start = (bf16[64,3072]{1,0:T(8,128)(2,1)S(1)}, bf16[64,3072]{1,0:T(8,128)(2,1)}, u32[]{:S(2)}) copy-start(bf16[64,3072]{1,0:T(8,128)(2,1)} %param.19) | copy-start | bytes 1179652
  2.4 1.2 %copy-start.1 = (bf16[2,8,128,256]{3,2,1,0:T(8,128)(2,1)S(1)}, bf16[2,8,128,256]{3,2,1,0:T(8,128)(2,1)}, u32[]{:S(2)}) copy-start(bf16[2,8,128,256]{3,2,1,0:T(8,128)(2,1)} %x_ref.1) | copy-start | bytes 3145732
  3.6 0.7 %copy-start.2 = (s32[3,8]{1,0:T(4,128)S(1)}, s32[3,8]{1,0:T(4,128)}, u32[]{:S(2)}) copy-start(s32[3,8]{1,0:T(4,128)} %maps_ref.1) | copy-start | bytes 292
  4.3 0.7 %copy-start.3 = (s32[2]{0:T(128)S(1)}, s32[2]{0:T(128)}, u32[]{:S(2)}) copy-start(s32[2]{0:T(128)} %clip_ref.1) | copy-start | bytes 28

commit v3 on v2

--- a/solution.py
+++ b/solution.py
@@ -8,7 +8,7 @@
 from jax.sharding import PartitionSpec as P
 
 MESH = pl.DeviceIdType.MESH
-ROW_BLOCK = 2
+ROW_BLOCK = 4
 
 
 def activate(values, gain_row):
@@ -20,14 +20,26 @@
 def encoder_kernel(
     clip_len,
     bands,
+    clip_hbm,
+    maps_hbm,
+    x_hbm,
+    g1_hbm,
+    g2_hbm,
+    g3_hbm,
+    lat_hbm,
+    w1_hbm,
+    w2_hbm,
+    fine_out,
+    mid_out,
+    coarse_out,
     clip_ref,
     maps_ref,
     x_ref,
-    gains_ref,
+    g1_ref,
+    g2_ref,
+    g3_ref,
+    lat_in,
     lat_ref,
-    w1_hbm,
-    w2_hbm,
-    out_ref,
     w_one,
     w_two,
     ext_one,
@@ -45,6 +57,7 @@
     stage,
     send_buf,
     recv_buf,
+    in_sem,
     w_sem,
     halo_send,
     halo_recv,
@@ -67,6 +80,20 @@
         ]
         for sec, (src, dst) in enumerate(((w1_hbm, w_one), (w2_hbm, w_two)))
     ]
+    pairs = (
+        (x_hbm, x_ref),
+        (g1_hbm, g1_ref),
+        (g2_hbm, g2_ref),
+        (g3_hbm, g3_ref),
+        (lat_hbm, lat_in),
+        (clip_hbm, clip_ref),
+        (maps_hbm, maps_ref),
+    )
+    small_copies = [
+        pltpu.make_async_copy(src, dst, in_sem.at[k]) for k, (src, dst) in enumerate(pairs)
+    ]
+    for copy in small_copies:
+        copy.start()
     for group in weight_copies:
         for copy in group:
             copy.start()
@@ -96,10 +123,6 @@
             device_id_type=MESH,
         )
 
-    gain_one = gains_ref[0:1, :]
-    gain_two = gains_ref[1:2, :]
-    gain_out = gains_ref[2:3, :]
-
     for ext in (ext_one, ext_two):
 
         @pl.when(jnp.logical_not(has_prev))
@@ -113,6 +136,26 @@
         @pl.when(jnp.logical_not(has_down))
         def _():
             ext[:, rows + 1] = jnp.zeros((frames + 2, cols, chans), jnp.bfloat16)
+
+    for copy in small_copies:
+        copy.wait()
+    gain_one = g1_ref[...]
+    gain_two = g2_ref[...]
+    gain_out = g3_ref[...]
+
+    lat_count = lat_in.shape[0]
+    spread_lane = lax.broadcasted_iota(jnp.int32, (lat_count, 128), 1)
+    spread_row = lax.broadcasted_iota(jnp.int32, (lat_count, 128), 0)
+    for f in range(frames):
+        hit = (lax.rem(spread_lane, lat_count) == spread_row) & (
+            lax.div(spread_lane, 64) == f
+        )
+        lat_ref[f] = lax.dot_general(
+            lat_in[...],
+            jnp.where(hit, 1.0, 0.0).astype(jnp.bfloat16),
+            (((0,), (0,)), ((), ())),
+            preferred_element_type=jnp.float32,
+        ).astype(jnp.bfloat16)
 
     @pl.loop(0, rows)
     def _(r):
@@ -304,24 +347,39 @@
         copy.wait_recv()
     for copy in moves:
         copy.wait_send()
-    out_ref[...] = recv_buf[...]
+    for d in range(bands):
+        got = recv_buf[d].astype(jnp.float32)
+        offset = 0
+        for out_ref in (fine_out, mid_out, coarse_out):
+            each = out_ref.shape[0] // bands
+            out_ref[d * each : (d + 1) * each] = got[offset : offset + each]
+            offset += each
 
 
 def encode(features, clip_frames, band_maps, gains, latents, conv_one, conv_two, clip_len):
     bands = lax.axis_size("space")
     frames, rows, cols, chans = features.shape
-    counts = [
-        (rows // s // 2, cols // s // 2) for s in (1, 2, 4)
-    ]
+    counts = [(rows // s // 2, cols // s // 2) for s in (1, 2, 4)]
     used = sum(n * w // bands for n, w in counts)
     message = -(-used // 16) * 16
     f32, bf16 = jnp.float32, jnp.bfloat16
     vmem = pl.BlockSpec(memory_space=pltpu.VMEM)
-    smem = pl.BlockSpec(memory_space=pltpu.SMEM)
-    hbm = pl.BlockSpec(memory_space=pl.ANY)
+    hbm = pl.BlockSpec(memory_space=pltpu.HBM)
     weight = pltpu.VMEM((3, 9, chans, chans), bf16)
     ext = pltpu.VMEM((frames + 2, rows + 2, cols, chans), bf16)
-    scratch = [weight, weight, ext, ext, pltpu.VMEM((frames, rows, cols, chans), bf16)]
+    stream = pltpu.VMEM((frames, rows, cols, chans), bf16)
+    gain = pltpu.VMEM((1, chans), f32)
+    scratch = [
+        pltpu.SMEM(clip_frames.shape, jnp.int32),
+        pltpu.SMEM(band_maps.shape, jnp.int32),
+        stream,
+        gain,
+        gain,
+        gain,
+        pltpu.VMEM(latents.shape, bf16),
+        pltpu.VMEM((frames, chans, 128), bf16),
+    ]
+    scratch += [weight, weight, ext, ext, stream]
     scratch.append(pltpu.VMEM((rows, cols, 128), f32))
     scratch += [pltpu.VMEM((n, w, 128), f32) for n, w in counts]
     scratch += [pltpu.VMEM((n, w, 128), f32) for n, w in counts[:2]]
@@ -330,6 +388,7 @@
         pltpu.VMEM((bands, message, 128), f32),
         pltpu.VMEM((bands, message, 128), bf16),
         pltpu.VMEM((bands, message, 128), bf16),
+        pltpu.SemaphoreType.DMA((7,)),
         pltpu.SemaphoreType.DMA((2, 3)),
         pltpu.SemaphoreType.DMA((2, 5)),
         pltpu.SemaphoreType.DMA((2, 5)),
@@ -338,15 +397,59 @@
     ]
     return pl.pallas_call(
         functools.partial(encoder_kernel, clip_len, bands),
-        out_shape=jax.ShapeDtypeStruct((bands, message, 128), bf16),
-        in_specs=[smem, smem, vmem, vmem, vmem, hbm, hbm],
-        out_specs=vmem,
+        out_shape=[jax.ShapeDtypeStruct((n * w, 128), f32) for n, w in counts],
+        in_specs=[hbm] * 9,
+        out_specs=[vmem] * 3,
         scratch_shapes=scratch,
         compiler_params=pltpu.CompilerParams(
-            collective_id=0, has_side_effects=True, vmem_limit_bytes=52 * 1024 * 1024
+            collective_id=0, has_side_effects=True, vmem_limit_bytes=63 * 1024 * 1024
         ),
         name="encoder",
-    )(clip_frames, band_maps, features, gains, latents, conv_one, conv_two)
+    )(clip_frames, band_maps, features, *gains, latents, conv_one, conv_two)
+
+
+def embed_kernel(fine_ref, mid_ref, coarse_ref, weight_ref, *out_refs):
+    weight = weight_ref[...]
+    blank = jnp.zeros_like(weight)
+    for f in range(out_refs[0].shape[0]):
+        halves = [blank, blank]
+        halves[f] = weight
+        padded = jnp.concatenate(halves, axis=0)
+        for source, out_ref in zip((fine_ref, mid_ref, coarse_ref), out_refs):
+            tokens = jnp.dot(
+                source[...].astype(jnp.bfloat16), padded, preferred_element_type=jnp.float32
+            )
+            _, _, token_rows, each, wide = out_ref.shape
+            if each % 8 == 0:
+                out_ref[f, 0] = tokens.reshape(token_rows, each, wide).astype(jnp.bfloat16)
+            else:
+                for i in range(token_rows):
+                    out_ref[f, 0, i] = tokens[i * each : (i + 1) * each].astype(jnp.bfloat16)
+
+
+def embed(patches, embed_weight, frames, bands, shapes):
+    depth, hidden = embed_weight.shape
+    steps = 4
+    wide = hidden // steps
+    whole = lambda h: (0, 0)
+    out_shape, out_specs = [], []
+    for token_rows, each in shapes:
+        out_shape.append(
+            jax.ShapeDtypeStruct((frames, 1, token_rows, each, hidden), jnp.bfloat16)
+        )
+        out_specs.append(
+            pl.BlockSpec((frames, 1, token_rows, each, wide), lambda h: (0, 0, 0, 0, h))
+        )
+    return pl.pallas_call(
+        embed_kernel,
+        grid=(steps,),
+        out_shape=out_shape,
+        in_specs=[pl.BlockSpec(p.shape, whole) for p in patches]
+        + [pl.BlockSpec((depth, wide), lambda h: (0, h))],
+        out_specs=out_specs,
+        compiler_params=pltpu.CompilerParams(vmem_limit_bytes=32 * 1024 * 1024),
+        name="embed",
+    )(*patches, embed_weight)
 
 
 def body(
@@ -364,38 +467,18 @@
     frames, rows, cols, chans = features.shape
     clip_len = frames * lax.axis_size("tm") // 2
     bands = lax.axis_size("space")
-    gains = jnp.stack([gain_one, gain_two, gain_out])
-    repeated = jnp.tile(latent_weight, (1, 4))
-    blank = jnp.zeros_like(repeated)
-    latents = jnp.stack(
-        [
-            jnp.concatenate([repeated, blank], axis=1),
-            jnp.concatenate([blank, repeated], axis=1),
-        ]
-    )
-    moved = encode(
+    patches = encode(
         features,
         clip_frames,
         band_maps,
-        gains,
-        latents,
+        [g.reshape(1, chans) for g in (gain_one, gain_two, gain_out)],
+        latent_weight.T,
         conv_one.reshape(9, 3, chans, chans),
         conv_two.reshape(9, 3, chans, chans),
         clip_len,
     )
-    depth = embed_weight.shape[0]
-    results = []
-    start = 0
-    for s in (1, 2, 4):
-        count, each = rows // s // 2, cols // s // 2 // bands
-        piece = moved[:, start : start + count * each]
-        start += count * each
-        piece = piece.reshape(bands * count, each, frames, depth).transpose(2, 0, 1, 3)
-        embedded = jnp.einsum(
-            "fice,eh->fich", piece, embed_weight, preferred_element_type=jnp.float32
-        ).astype(jnp.bfloat16)
-        results.append(embedded[:, None])
-    return tuple(results)
+    shapes = [(bands * (rows // s // 2), cols // s // 2 // bands) for s in (1, 2, 4)]
+    return tuple(embed(patches, embed_weight, frames, bands, shapes))
 
 
 def solution(mesh):

time: 56.6 us -> 52.7 us (0.931)
  Pallas kernels: 45.5 us -> 49.4 us
  local copies, waits for them, and re-layouts: 6.12 us -> 2.36 us
  matrix products: 3.16 us -> 0 us
  other arithmetic: 0.79 us -> 0 us
    pallas_call x0 -> x1, Pallas kernels: none -> 3.26 us  [embed(): pl.pallas_call(embed_kernel, grid=(steps,), out_shape=out_shape, in_specs...]
    dot_general x3 -> x0, matrix products: 3.16 us -> none  [body(): jnp.einsum('fice,eh->fich', piece, embed_weight, preferred_element_type=j...]
    unnamed x10 -> x8, local copies, waits for them, and re-layouts: 4.93 us -> 2.36 us
    another operation x3 -> x0, local copies, waits for them, and re-layouts: 0.91 us -> none  [the longest x2 0.81 us: body(): repeated = jnp.tile(latent_weight, (1, 4))]
    another operation x2 -> x0, other arithmetic: 0.79 us -> none  [the longest x1 0.77 us: body(): gains = jnp.stack([gain_one, gain_two, gain_out])]
    pallas_call x1, Pallas kernels: 45.5 us -> 46.1 us  [encode(): pl.pallas_call(functools.partial(encoder_kernel, clip_len, bands), out_sh...]
where the time goes in v3:
time: 52.7 us; the launch traced here: 52.4 us
  Pallas kernels  49.4 us (94%)
  local copies, waits for them, and re-layouts  2.36 us (4%)
  between operations  0.67 us (1%)
    pallas_call x1, Pallas kernels, encode(): pl.pallas_call(functools.partial(encoder_kernel, clip_len, bands), out_sh...  46.1 us
    pallas_call x1, Pallas kernels, embed(): pl.pallas_call(embed_kernel, grid=(steps,), out_shape=out_shape, in_specs...  3.26 us
    unnamed x8, local copies, waits for them, and re-layouts  2.36 us

profile of v3, /device:TPU:1, one launch (start us, length us, event | category | flops | bytes accessed | tf_op | source)
XLA Modules:
  0.0 52.4 jit_solution(12369394552790492091)
XLA Ops:
  0.6 0.0 copy-start
  0.6 46.1 %encoder.1 = (f32[256,128]{1,0:T(8,128)}, f32[64,128]{1,0:T(8,128)}, f32[16,128]{1,0:T(8,128)}) custom-call(s32[2]{0:T(128)} %clip_hbm.1, s32[3,8]{1,0:T(4,128)} %maps_hbm.1, bf16[2,8,128,256]{3,2,1,0:T(8,128)(2,1)} %x_hbm.1, f32[1,256]{1,0:T(1,128)} %bitcast.9, f32[1,256]{1,0:T(1,128)} %bitcast.10, f32[1,256]{1,0:T(1,128)} %bitcast.11, ...), custom_call_target="tpu_custom_call" | custom-call | tf_op jit(solution)/shard_map/encoder/pallas_call | solution.py:398
  46.8 0.0 copy-done
  46.8 0.0 copy-start.1
  46.8 0.9 %copy-done.1 = f32[256,128]{1,0:T(8,128)S(1)} copy-done((f32[256,128]{1,0:T(8,128)S(1)}, f32[256,128]{1,0:T(8,128)}, u32[]{:S(2)}) %copy-start.1) | copy-done | bytes 131096
  47.7 0.0 copy-start.2
  47.7 0.8 %copy-done.2 = f32[64,128]{1,0:T(8,128)S(1)} copy-done((f32[64,128]{1,0:T(8,128)S(1)}, f32[64,128]{1,0:T(8,128)}, u32[]{:S(2)}) %copy-start.2) | copy-done | bytes 32792
  48.5 0.0 copy-start.3
  48.5 0.7 %copy-done.3 = f32[16,128]{1,0:T(8,128)S(1)} copy-done((f32[16,128]{1,0:T(8,128)S(1)}, f32[16,128]{1,0:T(8,128)}, u32[]{:S(2)}) %copy-start.3) | copy-done | bytes 8216
  49.2 3.3 %embed.1 = (bf16[2,1,32,8,3072]{4,3,2,1,0:T(8,128)(2,1)}, bf16[2,1,16,4,3072]{4,3,2,1,0:T(4,128)(2,1)}, bf16[2,1,8,2,3072]{4,3,2,1,0:T(2,128)(2,1)}) custom-call(f32[256,128]{1,0:T(8,128)S(1)} %copy-done.1, f32[64,128]{1,0:T(8,128)S(1)} %copy-done.2, f32[16,128]{1,0:T(8,128)S(1)} %copy-done.3, bf16[64,3072]{1,0:T(8,128)(2,1)S(1)} %copy-done), custom_call_target="tpu_custom_call" | custom-call | tf_op jit(solution)/shard_map/embed/pallas_call | solution.py:443
Async XLA Ops:
  0.6 46.2 %copy-start = (bf16[64,3072]{1,0:T(8,128)(2,1)S(1)}, bf16[64,3072]{1,0:T(8,128)(2,1)}, u32[]{:S(2)}) copy-start(bf16[64,3072]{1,0:T(8,128)(2,1)} %weight_ref.1) | copy-start | bytes 1179652
  46.8 0.9 %copy-start.1 = (f32[256,128]{1,0:T(8,128)S(1)}, f32[256,128]{1,0:T(8,128)}, u32[]{:S(2)}) copy-start(f32[256,128]{1,0:T(8,128)} %get-tuple-element.6.fine_ref) | copy-start | bytes 393220
  47.7 0.8 %copy-start.2 = (f32[64,128]{1,0:T(8,128)S(1)}, f32[64,128]{1,0:T(8,128)}, u32[]{:S(2)}) copy-start(f32[64,128]{1,0:T(8,128)} %get-tuple-element.7.mid_ref) | copy-start | bytes 98308
  48.5 0.7 %copy-start.3 = (f32[16,128]{1,0:T(8,128)S(1)}, f32[16,128]{1,0:T(8,128)}, u32[]{:S(2)}) copy-start(f32[16,128]{1,0:T(8,128)} %get-tuple-element.8.coarse_ref) | copy-start | bytes 24580

commit v4 on v3

--- a/solution.py
+++ b/solution.py
@@ -8,8 +8,6 @@
 from jax.sharding import PartitionSpec as P
 
 MESH = pl.DeviceIdType.MESH
-ROW_BLOCK = 4
-
 
 def activate(values, gain_row):
     meansq = jnp.mean(values * values, axis=-1, keepdims=True)
@@ -157,11 +155,13 @@
             preferred_element_type=jnp.float32,
         ).astype(jnp.bfloat16)
 
-    @pl.loop(0, rows)
-    def _(r):
+    def activate_row(r):
         for f in range(frames):
             values = x_ref[f, r].astype(jnp.float32)
             ext_one[2 + f, r + 1] = activate(values, gain_one).astype(jnp.bfloat16)
+
+    activate_row(0)
+    activate_row(rows - 1)
 
     peers = bands - 1
     for there, _, _ in links:
@@ -169,14 +169,27 @@
     pl.semaphore_wait(barrier, peers)
 
     def halo(sec, ext):
+        last, own = slice(frames, frames + 2), slice(2, frames + 2)
+        old = slice(0, 2)
+        low, high = rows, rows + 1
         sends = (
-            (has_next, ext.at[frames : frames + 2, 1 : rows + 1], ext.at[0:2, 1 : rows + 1], 1, 0),
-            (has_up, ext.at[2 : frames + 2, 1], ext.at[2 : frames + 2, rows + 1], 0, -1),
-            (has_down, ext.at[2 : frames + 2, rows], ext.at[2 : frames + 2, 0], 0, 1),
-            (has_next & has_up, ext.at[frames : frames + 2, 1], ext.at[0:2, rows + 1], 1, -1),
-            (has_next & has_down, ext.at[frames : frames + 2, rows], ext.at[0:2, 0], 1, 1),
-        )
-        waits = (has_prev, has_down, has_up, has_prev & has_down, has_prev & has_up)
+            (has_next, ext.at[last, 2:rows], ext.at[old, 2:rows], 1, 0),
+            (has_up, ext.at[own, 1], ext.at[own, high], 0, -1),
+            (has_down, ext.at[own, low], ext.at[own, 0], 0, 1),
+            (has_next & has_up, ext.at[last, 1], ext.at[old, high], 1, -1),
+            (has_next & has_down, ext.at[last, low], ext.at[old, 0], 1, 1),
+            (has_next, ext.at[last, 1], ext.at[old, 1], 1, 0),
+            (has_next, ext.at[last, low], ext.at[old, low], 1, 0),
+        )
+        waits = (
+            has_prev,
+            has_down,
+            has_up,
+            has_prev & has_down,
+            has_prev & has_up,
+            has_prev,
+            has_prev,
+        )
         made = []
         for k, (there, src, dst, dt, ds) in enumerate(sends):
             copy = pltpu.make_async_remote_copy(
@@ -190,16 +203,17 @@
             made.append((there, waits[k], copy))
         return made
 
-    def start_all(made):
-        for k in (1, 2, 3, 4, 0):
+    def start(made, which):
+        for k in which:
             there, _, copy = made[k]
 
             @pl.when(there)
             def _():
                 copy.start()
 
-    def finish_recv(made):
-        for _, here, copy in made:
+    def finish_recv(made, which):
+        for k in which:
+            _, here, copy = made[k]
 
             @pl.when(here)
             def _():
@@ -213,12 +227,15 @@
                 copy.wait_send()
 
     col_id = lax.broadcasted_iota(jnp.int32, (cols, chans), 0)
-    size = ROW_BLOCK * cols
-
-    def conv_rows(ext, weight, r0, f):
+    interior = rows - 2
+    row_block = max(n for n in (1, 2, 3) if interior % n == 0)
+    ends = (0, rows - 1)
+    inner, edges, across = (0,), (1, 2, 3, 4, 5, 6), (1, 2, 3, 4)
+
+    def conv_rows(ext, weight, which, f):
         lhs = jnp.concatenate(
             [
-                ext[f + kt, pl.ds(r0 + ky, ROW_BLOCK)].reshape(size, chans)
+                jnp.concatenate([ext[f + kt, r + ky] for r in which], axis=0)
                 for kt in range(3)
                 for ky in range(3)
             ],
@@ -233,52 +250,65 @@
             for kx in range(3)
         ]
         done = []
-        for k in range(ROW_BLOCK):
+        for k in range(len(which)):
             left, mid, right = (tap[k * cols : (k + 1) * cols] for tap in taps)
             left = jnp.where(col_id == 0, 0.0, pltpu.roll(left, 1, 0))
             right = jnp.where(col_id == cols - 1, 0.0, pltpu.roll(right, cols - 1, 0))
             done.append(mid + left + right)
         return done
 
-    halo_one = halo(0, ext_one)
-    start_all(halo_one)
-    for copy in weight_copies[0]:
-        copy.wait()
-    finish_recv(halo_one)
-
-    @pl.loop(0, rows // ROW_BLOCK)
-    def _(block):
-        r0 = block * ROW_BLOCK
+    def first_section(which):
         for f in range(frames):
-            for k, update in enumerate(conv_rows(ext_one, w_one, r0, f)):
-                total = x_ref[f, r0 + k].astype(jnp.float32) + update
+            for r, update in zip(which, conv_rows(ext_one, w_one, which, f)):
+                total = x_ref[f, r].astype(jnp.float32) + update
                 rounded = total.astype(jnp.bfloat16)
-                mid_stream[f, r0 + k] = rounded
-                ext_two[2 + f, r0 + k + 1] = activate(
+                mid_stream[f, r] = rounded
+                ext_two[2 + f, r + 1] = activate(
                     rounded.astype(jnp.float32), gain_two
                 ).astype(jnp.bfloat16)
 
-    halo_two = halo(1, ext_two)
-    start_all(halo_two)
-    for copy in weight_copies[1]:
-        copy.wait()
-    finish_recv(halo_two)
-
-    @pl.loop(0, rows // ROW_BLOCK)
-    def _(block):
-        r0 = block * ROW_BLOCK
-        latents = [jnp.zeros((cols, 128), jnp.float32)] * ROW_BLOCK
+    def second_section(which):
+        latents = [jnp.zeros((cols, 128), jnp.float32) for _ in which]
         for f in range(frames):
-            for k, update in enumerate(conv_rows(ext_two, w_two, r0, f)):
-                total = mid_stream[f, r0 + k].astype(jnp.float32) + update
+            for k, update in enumerate(conv_rows(ext_two, w_two, which, f)):
+                total = mid_stream[f, which[k]].astype(jnp.float32) + update
                 final = activate(
                     total.astype(jnp.bfloat16).astype(jnp.float32), gain_out
                 ).astype(jnp.bfloat16)
                 latents[k] = latents[k] + jnp.dot(
                     final, lat_ref[f], preferred_element_type=jnp.float32
                 )
-        for k in range(ROW_BLOCK):
-            lat_rows[r0 + k] = latents[k]
+        for r, latent in zip(which, latents):
+            lat_rows[r] = latent
+
+    def interior_rows(section):
+        @pl.loop(0, interior // row_block)
+        def _(block):
+            section([1 + block * row_block + k for k in range(row_block)])
+
+    halo_one = halo(0, ext_one)
+    halo_two = halo(1, ext_two)
+    start(halo_one, edges)
+
+    @pl.loop(1, rows - 1)
+    def _(r):
+        activate_row(r)
+
+    start(halo_one, inner)
+    for copy in weight_copies[0]:
+        copy.wait()
+    finish_recv(halo_one, (0, 5, 6))
+    interior_rows(first_section)
+    start(halo_two, inner)
+    finish_recv(halo_one, across)
+    first_section(ends)
+    start(halo_two, edges)
+    for copy in weight_copies[1]:
+        copy.wait()
+    finish_recv(halo_two, (0, 5, 6))
+    interior_rows(second_section)
+    finish_recv(halo_two, across)
+    second_section(ends)
 
     finish_send(halo_one)
     finish_send(halo_two)
@@ -390,8 +420,8 @@
         pltpu.VMEM((bands, message, 128), bf16),
         pltpu.SemaphoreType.DMA((7,)),
         pltpu.SemaphoreType.DMA((2, 3)),
-        pltpu.SemaphoreType.DMA((2, 5)),
-        pltpu.SemaphoreType.DMA((2, 5)),
+        pltpu.SemaphoreType.DMA((2, 7)),
+        pltpu.SemaphoreType.DMA((2, 7)),
         pltpu.SemaphoreType.DMA((bands - 1,)),
         pltpu.SemaphoreType.DMA((bands - 1,)),
     ]
@@ -447,7 +477,7 @@
         in_specs=[pl.BlockSpec(p.shape, whole) for p in patches]
         + [pl.BlockSpec((depth, wide), lambda h: (0, h))],
         out_specs=out_specs,
-        compiler_params=pltpu.CompilerParams(vmem_limit_bytes=32 * 1024 * 1024),
+        compiler_params=pltpu.CompilerParams(vmem_limit_bytes=63 * 1024 * 1024),
         name="embed",
     )(*patches, embed_weight)
 

time: 52.7 us -> 38.4 us (0.73)
  Pallas kernels: 49.4 us -> 37.6 us
  local copies, waits for them, and re-layouts: 2.36 us -> 0 us
    pallas_call x1, Pallas kernels: 46.1 us -> 32.9 us  [encode(): pl.pallas_call(functools.partial(encoder_kernel, clip_len, bands), out_sh...]
    unnamed x8 -> x0, local copies, waits for them, and re-layouts: 2.36 us -> none
    pallas_call x1, Pallas kernels: 3.26 us -> 4.69 us  [embed(): pl.pallas_call(embed_kernel, grid=(steps,), out_shape=out_shape, in_specs...]
where the time goes in v4:
time: 38.4 us; the launch traced here: 38.2 us
  Pallas kernels  37.6 us (98%)
  between operations  0.64 us (2%)
    pallas_call x1, Pallas kernels, encode(): pl.pallas_call(functools.partial(encoder_kernel, clip_len, bands), out_sh...  32.9 us
    pallas_call x1, Pallas kernels, embed(): pl.pallas_call(embed_kernel, grid=(steps,), out_shape=out_shape, in_specs...  4.69 us

profile of v4, /device:TPU:1, one launch (start us, length us, event | category | flops | bytes accessed | tf_op | source)
XLA Modules:
  0.0 38.2 jit_solution(8362675934086877220)
XLA Ops:
  0.6 32.9 %encoder.1 = (f32[256,128]{1,0:T(8,128)}, f32[64,128]{1,0:T(8,128)}, f32[16,128]{1,0:T(8,128)}) custom-call(s32[2]{0:T(128)} %clip_hbm.1, s32[3,8]{1,0:T(4,128)} %maps_hbm.1, bf16[2,8,128,256]{3,2,1,0:T(8,128)(2,1)} %x_hbm.1, f32[1,256]{1,0:T(1,128)} %bitcast.9, f32[1,256]{1,0:T(1,128)} %bitcast.10, f32[1,256]{1,0:T(1,128)} %bitcast.11, ...), custom_call_target="tpu_custom_call" | custom-call | tf_op jit(solution)/shard_map/encoder/pallas_call | solution.py:428
  33.5 4.7 %embed.1 = (bf16[2,1,32,8,3072]{4,3,2,1,0:T(8,128)(2,1)}, bf16[2,1,16,4,3072]{4,3,2,1,0:T(4,128)(2,1)}, bf16[2,1,8,2,3072]{4,3,2,1,0:T(2,128)(2,1)}) custom-call(f32[256,128]{1,0:T(8,128)} %get-tuple-element.6.fine_ref, f32[64,128]{1,0:T(8,128)} %get-tuple-element.7.mid_ref, f32[16,128]{1,0:T(8,128)} %get-tuple-element.8.coarse_ref, bf16[64,3072]{1,0:T(8,128)(2,1)} %weight_ref.1), custom_call_target="tpu_custom_call" | custom-call | tf_op jit(solution)/shard_map/embed/pallas_call | solution.py:473

commit v5 on v4

--- a/solution.py
+++ b/solution.py
@@ -228,7 +228,7 @@
 
     col_id = lax.broadcasted_iota(jnp.int32, (cols, chans), 0)
     interior = rows - 2
-    row_block = max(n for n in (1, 2, 3) if interior % n == 0)
+    row_block = max(n for n in (1, 2, 3, 6) if interior % n == 0)
     ends = (0, rows - 1)
     inner, edges, across = (0,), (1, 2, 3, 4, 5, 6), (1, 2, 3, 4)
 

time: 38.4 us -> 38.4 us (level)
  no operation moved by 1% of the time
where the time goes in v5:
time: 38.4 us; the launch traced here: 38.2 us
  Pallas kernels  37.5 us (98%)
  between operations  0.64 us (2%)
    pallas_call x1, Pallas kernels, encode(): pl.pallas_call(functools.partial(encoder_kernel, clip_len, bands), out_sh...  32.9 us
    pallas_call x1, Pallas kernels, embed(): pl.pallas_call(embed_kernel, grid=(steps,), out_shape=out_shape, in_specs...  4.68 us

profile of v5, /device:TPU:1, one launch (start us, length us, event | category | flops | bytes accessed | tf_op | source)
XLA Modules:
  0.0 38.2 jit_solution(17475435993210916965)
XLA Ops:
  0.6 32.9 %encoder.1 = (f32[256,128]{1,0:T(8,128)}, f32[64,128]{1,0:T(8,128)}, f32[16,128]{1,0:T(8,128)}) custom-call(s32[2]{0:T(128)} %clip_hbm.1, s32[3,8]{1,0:T(4,128)} %maps_hbm.1, bf16[2,8,128,256]{3,2,1,0:T(8,128)(2,1)} %x_hbm.1, f32[1,256]{1,0:T(1,128)} %bitcast.9, f32[1,256]{1,0:T(1,128)} %bitcast.10, f32[1,256]{1,0:T(1,128)} %bitcast.11, ...), custom_call_target="tpu_custom_call" | custom-call | tf_op jit(solution)/shard_map/encoder/pallas_call | solution.py:428
  33.5 4.7 %embed.1 = (bf16[2,1,32,8,3072]{4,3,2,1,0:T(8,128)(2,1)}, bf16[2,1,16,4,3072]{4,3,2,1,0:T(4,128)(2,1)}, bf16[2,1,8,2,3072]{4,3,2,1,0:T(2,128)(2,1)}) custom-call(f32[256,128]{1,0:T(8,128)} %get-tuple-element.6.fine_ref, f32[64,128]{1,0:T(8,128)} %get-tuple-element.7.mid_ref, f32[16,128]{1,0:T(8,128)} %get-tuple-element.8.coarse_ref, bf16[64,3072]{1,0:T(8,128)(2,1)} %weight_ref.1), custom_call_target="tpu_custom_call" | custom-call | tf_op jit(solution)/shard_map/embed/pallas_call | solution.py:473
